TPU v7x, 32 devices: a whole 2x2x4 slice. The times are simulated.
32 devices in a mesh: dp: 4 (over y, x), tensor: 8 (over z, core).
Axes of the slice: x: 2, y: 2, z: 4, core: 2. Of those that a mesh axis runs over, the one named last changes fastest.
Arguments:
- inputs: bfloat16 [4, 2048, 2048], P('dp'), may hold values from -6 to 6
- segment_ids: int32 [4, 2048], P('dp'), may hold values from 0 to 7, never falling along the last dimension, each value on 1 to 1024 neighbouring positions
- norm_gain: bfloat16 [2048], replicated, may hold values from 0.5 to 1.5
- norm_bias: bfloat16 [2048], replicated, may hold values from -2 to 2
- qkv_weight: bfloat16 [2048, 3, 2048], P(None, None, 'tensor'), may hold values from -0.125 to 0.125
- qkv_bias: bfloat16 [3, 2048], P(None, 'tensor'), may hold values from -2 to 2
- out_weight: bfloat16 [2048, 2048], P('tensor'), may hold values from -0.5 to 0.5
- out_bias: bfloat16 [2048], replicated, may hold values from -2 to 2
- up_weight: bfloat16 [2048, 8192], P(None, 'tensor'), may hold values from -0.125 to 0.125
- up_bias: bfloat16 [8192], P('tensor'), may hold values from -2 to 2
- down_weight: bfloat16 [8192, 2048], P('tensor'), may hold values from -0.0625 to 0.0625
- down_bias: bfloat16 [2048], replicated, may hold values from -2 to 2
- cotangent: bfloat16 [4, 2048, 2048], P('dp'), may hold values from -6 to 6
Outputs:
- output: bfloat16 [4, 2048, 2048], P('dp')
- input_grad: bfloat16 [4, 2048, 2048], P('dp')
- norm_gain_grad: float32 [2048], P('dp')
- norm_bias_grad: float32 [2048], P('dp')
- qkv_weight_grad: float32 [2048, 3, 2048], P('dp', None, 'tensor')
- qkv_bias_grad: float32 [3, 32, 64], P(None, 'tensor', 'dp')
- out_weight_grad: float32 [2048, 2048], P('tensor', 'dp')
- out_bias_grad: float32 [2048], P('dp')
- up_weight_grad: float32 [2048, 8192], P('dp', 'tensor')
- up_bias_grad: float32 [128, 64], P('tensor', 'dp')
- down_weight_grad: float32 [8192, 2048], P('tensor', 'dp')
- down_bias_grad: float32 [2048], P('dp')
Inputs may be any that keep to these rules, and one draw needn't show every extreme that they name: `segment_ids`: along each row the ids never fall; every document holds 1 to 1024 tokens, and one document of each row holds exactly 1024.
All inputs are finite; a program needn't handle non-finite values.
Results may differ from a plain program's by a relative error of at most 0.017.
Values may be sent and summed in bfloat16 or wider, within the bound.
A program may use at most 256 MiB of HBM per device.

v0:
```python
from functools import partial

import jax
import jax.numpy as jnp
from jax import lax
from jax.sharding import PartitionSpec as P

D = 2048
HD = 64
ROT = 32


def positions_of(segment_row):
    length = segment_row.shape[0]
    places = jnp.arange(length, dtype=jnp.int32)
    earlier = jnp.concatenate([segment_row[:1] - 1, segment_row[:-1]])
    starts = jnp.where(segment_row != earlier, places, jnp.zeros_like(places))
    return places - lax.cummax(starts, axis=0)


def rotary_tables(segment_row):
    places = positions_of(segment_row).astype(jnp.float32)
    freqs = 10000.0 ** (-jnp.arange(ROT // 2, dtype=jnp.float32) * 2.0 / ROT)
    angles = places[:, None] * freqs[None, :]
    return (jnp.cos(angles), jnp.sin(angles))


def rotate(vectors, cosine, sine):
    first = vectors[..., : ROT // 2]
    second = vectors[..., ROT // 2 : ROT]
    cos_wide = cosine[:, None, :]
    sin_wide = sine[:, None, :]
    return jnp.concatenate(
        [
            first * cos_wide - second * sin_wide,
            second * cos_wide + first * sin_wide,
            vectors[..., ROT:],
        ],
        axis=-1,
    )


def contract_rows(left, right):
    return lax.dot_general(
        left, right, (((0,), (0,)), ((), ())), preferred_element_type=jnp.float32
    )


def times_transposed(left, right):
    return lax.dot_general(
        left, right, (((1,), (1,)), ((), ())), preferred_element_type=jnp.float32
    )


def norm_parts(values):
    average = jnp.mean(values, axis=-1, keepdims=True)
    centered = values - average
    inverse = lax.rsqrt(jnp.mean(centered * centered, axis=-1, keepdims=True) + 1e-05)
    return (centered * inverse, inverse)


def norm_backward(grad_normed, scaled, inverse, gain_float):
    grad_hat = grad_normed * gain_float
    return inverse * (
        grad_hat
        - jnp.mean(grad_hat, axis=-1, keepdims=True)
        - scaled * jnp.mean(grad_hat * scaled, axis=-1, keepdims=True)
    )


def block_mask(segment_row, block_start, block_rows):
    places = jnp.arange(segment_row.shape[0], dtype=jnp.int32)
    q_segment = lax.dynamic_slice_in_dim(segment_row, block_start, block_rows, 0)
    q_place = lax.dynamic_slice_in_dim(places, block_start, block_rows, 0)
    return (q_segment[:, None] == segment_row[None, :]) & (q_place[:, None] >= places[None, :])


def attention_forward(queries, keys, values, segment_row):
    length, heads_here, head_dim = queries.shape
    block_rows = min(512, length)
    scaling = head_dim ** (-0.5)

    def one_block(block_index):
        block_start = block_index * block_rows
        q_block = lax.dynamic_slice_in_dim(queries, block_start, block_rows, 0)
        allowed = block_mask(segment_row, block_start, block_rows)
        scores = (
            jnp.einsum("qhd,khd->hqk", q_block, keys, preferred_element_type=jnp.float32) * scaling
        )
        scores = jnp.where(allowed[None], scores, -1e30)
        row_max = jnp.max(scores, axis=-1, keepdims=True)
        raised = jnp.exp(scores - row_max)
        total = jnp.sum(raised, axis=-1, keepdims=True)
        weights = (raised / total).astype(jnp.bfloat16)
        mixed = jnp.einsum("hqk,khd->qhd", weights, values, preferred_element_type=jnp.float32)
        return (mixed.astype(jnp.bfloat16), (row_max + jnp.log(total))[..., 0])

    mixed, logsum = lax.map(one_block, jnp.arange(length // block_rows))
    return (mixed.reshape(length, heads_here * head_dim), logsum)


def attention_backward(queries, keys, values, segment_row, grad_mixed, logsum):
    length, heads_here, head_dim = queries.shape
    block_rows = min(512, length)
    scaling = head_dim ** (-0.5)

    def one_block(carry, block_index):
        grad_keys, grad_values = carry
        block_start = block_index * block_rows
        q_block = lax.dynamic_slice_in_dim(queries, block_start, block_rows, 0)
        do_block = lax.dynamic_slice_in_dim(grad_mixed, block_start, block_rows, 0)
        allowed = block_mask(segment_row, block_start, block_rows)
        scores = (
            jnp.einsum("qhd,khd->hqk", q_block, keys, preferred_element_type=jnp.float32) * scaling
        )
        shifted = jnp.where(allowed[None], scores - logsum[block_index][:, :, None], -1e30)
        probability = jnp.exp(shifted)
        grad_prob = jnp.einsum("qhd,khd->hqk", do_block, values, preferred_element_type=jnp.float32)
        grad_scores = (
            probability * (grad_prob - jnp.sum(probability * grad_prob, axis=-1, keepdims=True))
        ).astype(jnp.bfloat16)
        grad_q = (
            jnp.einsum("hqk,khd->qhd", grad_scores, keys, preferred_element_type=jnp.float32)
            * scaling
        )
        grad_keys = (
            grad_keys
            + jnp.einsum("hqk,qhd->khd", grad_scores, q_block, preferred_element_type=jnp.float32)
            * scaling
        )
        grad_values = grad_values + jnp.einsum(
            "hqk,qhd->khd",
            probability.astype(jnp.bfloat16),
            do_block,
            preferred_element_type=jnp.float32,
        )
        return ((grad_keys, grad_values), grad_q)

    empty = jnp.zeros((length, heads_here, head_dim), jnp.float32)
    (grad_keys, grad_values), grad_queries = lax.scan(
        one_block, (empty, empty), jnp.arange(length // block_rows)
    )
    return (grad_queries.reshape(length, heads_here, head_dim), grad_keys, grad_values)


def on_device(
    inputs,
    segment_ids,
    norm_gain,
    norm_bias,
    qkv_weight,
    qkv_bias,
    out_weight,
    out_bias,
    up_weight,
    up_bias,
    down_weight,
    down_bias,
    cotangent,
):
    inputs_row = inputs[0].astype(jnp.float32)
    segment_row = segment_ids[0]
    length = inputs_row.shape[0]
    local_width = qkv_weight.shape[2]
    heads_here = local_width // HD
    cosine, sine = rotary_tables(segment_row)
    gain_float = norm_gain.astype(jnp.float32)
    scaled, inverse = norm_parts(inputs_row)
    normed = (scaled * gain_float + norm_bias.astype(jnp.float32)).astype(jnp.bfloat16)
    qkv_matrix = qkv_weight.reshape(D, 3 * local_width)
    packed = (
        jnp.dot(normed, qkv_matrix, preferred_element_type=jnp.float32).reshape(
            length, 3, local_width
        )
        + qkv_bias.astype(jnp.float32)[None]
    )
    packed = packed.reshape(length, 3, heads_here, HD)
    queries = rotate(packed[:, 0], cosine, sine).astype(jnp.bfloat16)
    keys = rotate(packed[:, 1], cosine, sine).astype(jnp.bfloat16)
    values = packed[:, 2].astype(jnp.bfloat16)
    mixed, logsum = attention_forward(queries, keys, values, segment_row)
    hidden_pre = jnp.dot(normed, up_weight, preferred_element_type=jnp.float32) + up_bias.astype(
        jnp.float32
    )
    hidden = jax.nn.gelu(hidden_pre, approximate=True).astype(jnp.bfloat16)
    partial_sum = jnp.dot(mixed, out_weight, preferred_element_type=jnp.float32) + jnp.dot(
        hidden, down_weight, preferred_element_type=jnp.float32
    )
    biases = out_bias.astype(jnp.float32) + down_bias.astype(jnp.float32)
    summed = lax.psum(partial_sum.astype(jnp.bfloat16), "tensor").astype(jnp.float32)
    output = (inputs_row + summed + biases).astype(jnp.bfloat16)
    grad_out = cotangent[0]
    grad_bias_sum = jnp.sum(grad_out, axis=0, dtype=jnp.float32)
    grad_down = contract_rows(hidden, grad_out)
    grad_out_weight = contract_rows(mixed, grad_out)
    grad_hidden = times_transposed(grad_out, down_weight)
    gelu_value, gelu_pullback = jax.vjp(partial(jax.nn.gelu, approximate=True), hidden_pre)
    grad_pre = gelu_pullback(grad_hidden)[0].astype(jnp.bfloat16)
    grad_up = contract_rows(normed, grad_pre)
    grad_up_bias = jnp.sum(grad_pre, axis=0, dtype=jnp.float32).reshape(-1, HD)
    grad_normed = times_transposed(grad_pre, up_weight)
    grad_mixed = (
        times_transposed(grad_out, out_weight).astype(jnp.bfloat16).reshape(length, heads_here, HD)
    )
    grad_queries, grad_keys, grad_values = attention_backward(
        queries, keys, values, segment_row, grad_mixed, logsum
    )
    grad_packed = jnp.stack(
        [rotate(grad_queries, cosine, -sine), rotate(grad_keys, cosine, -sine), grad_values], axis=1
    )
    grad_packed = grad_packed.astype(jnp.bfloat16).reshape(length, 3 * local_width)
    grad_qkv = contract_rows(normed, grad_packed).reshape(D, 3, local_width)
    grad_qkv_bias = jnp.sum(grad_packed, axis=0, dtype=jnp.float32).reshape(3, heads_here, HD)
    grad_normed = grad_normed + times_transposed(grad_packed, qkv_matrix)
    grad_whole = lax.psum(grad_normed.astype(jnp.bfloat16), "tensor").astype(jnp.float32)
    input_grad = (
        grad_out.astype(jnp.float32) + norm_backward(grad_whole, scaled, inverse, gain_float)
    ).astype(jnp.bfloat16)
    grad_gain = jnp.sum(grad_whole * scaled, axis=0)
    grad_shift = jnp.sum(grad_whole, axis=0)
    all_shares = (
        lax.psum_scatter(
            grad_out_weight.astype(jnp.bfloat16), "dp", scatter_dimension=1, tiled=True
        ).astype(jnp.float32),
        lax.psum_scatter(
            grad_bias_sum.astype(jnp.bfloat16), "dp", scatter_dimension=0, tiled=True
        ).astype(jnp.float32),
        lax.psum_scatter(
            grad_up.astype(jnp.bfloat16), "dp", scatter_dimension=0, tiled=True
        ).astype(jnp.float32),
        lax.psum_scatter(
            grad_up_bias.astype(jnp.bfloat16), "dp", scatter_dimension=1, tiled=True
        ).astype(jnp.float32),
        lax.psum_scatter(
            grad_down.astype(jnp.bfloat16), "dp", scatter_dimension=1, tiled=True
        ).astype(jnp.float32),
        lax.psum_scatter(
            grad_qkv.astype(jnp.bfloat16), "dp", scatter_dimension=0, tiled=True
        ).astype(jnp.float32),
        lax.psum_scatter(
            grad_qkv_bias.astype(jnp.bfloat16), "dp", scatter_dimension=2, tiled=True
        ).astype(jnp.float32),
        lax.psum_scatter(
            grad_gain.astype(jnp.bfloat16), "dp", scatter_dimension=0, tiled=True
        ).astype(jnp.float32),
        lax.psum_scatter(
            grad_shift.astype(jnp.bfloat16), "dp", scatter_dimension=0, tiled=True
        ).astype(jnp.float32),
    )
    mlp_shares = all_shares[:5]
    attn_shares = all_shares[5:]
    out_w_share, bias_share, up_w_share, up_b_share, down_w_share = mlp_shares
    qkv_w_share, qkv_b_share, gain_share, shift_share = attn_shares
    return (
        output[None],
        input_grad[None],
        gain_share,
        shift_share,
        qkv_w_share,
        qkv_b_share,
        out_w_share,
        bias_share,
        up_w_share,
        up_b_share,
        down_w_share,
        bias_share,
    )


def solution(mesh):
    placed = (
        P("dp", None, None),
        P("dp", None),
        P(),
        P(),
        P(None, None, "tensor"),
        P(None, "tensor"),
        P("tensor", None),
        P(),
        P(None, "tensor"),
        P("tensor"),
        P("tensor", None),
        P(),
        P("dp", None, None),
    )
    return jax.shard_map(
        on_device,
        mesh=mesh,
        in_specs=placed,
        out_specs=(
            P("dp", None, None),
            P("dp", None, None),
            P("dp"),
            P("dp"),
            P("dp", None, "tensor"),
            P(None, "tensor", "dp"),
            P("tensor", "dp"),
            P("dp"),
            P("dp", "tensor"),
            P("tensor", "dp"),
            P("tensor", "dp"),
            P("dp"),
        ),
        check_vma=False,
    )
```

profile of v0, /device:TPU:5, one launch (start us, length us, event | category | flops | bytes accessed | tf_op | source)
XLA Modules:
  0.0 975.0 jit_solution(9115111842442903243)
XLA Ops:
  46.7 74.4 %while.27 = (s32[]{:T(128)}, bf16[4,512,4,64]{1,3,2,0:T(8,128)(2,1)}, f32[4,4,512]{2,1,0:T(4,128)}, s32[4]{0:T(128)S(1)}, s32[2048]{0:T(1024)S(1)}, /*index=5*/s...) while((s32[]{:T(128)}, ...), condition=%wide.region_7.8_spmd, body=%wide.region_4.7_spmd.sunk | while | flops 1127348736 | bytes 57232576 | solution.py:98
  138.0 333.4 %while.28 = (s32[]{:T(128)}, f32[2048,4,64]{0,2,1:T(8,128)}, f32[2048,4,64]{0,2,1:T(8,128)}, f32[4,512,4,64]{1,0,3,2:T(4,128)}, s32[4]{0:T(128)S(1)}, /*index=5*...) while((s32[]{:T(128)}, f32[2048,4,64]{0,2,1:T(8,128)}, ...), condition=%wide.region_11.12_spmd.clone, body=%wide.region_9.11_spmd.clone.sunk | while | flops 2753165824 | bytes 208284176 | solution.py:140
  164.1 15.8 %multiply_reduce_fusion.2 = (f32[4,512]{1,0:T(4,128)}, f32[4,512,2048]{2,1,0:T(8,128)}) fusion(f32[4,512,2048]{2,1,0:T(8,128)} %fusion.160, f32[4,512]{1,0:T(4,128)S(1)} %dynamic-slice_bitcast_fusion.2, pred[512,2048]{1,0:T(8,128)(4,1)} %fusion.161, bf16[2048,4,64]{0,2,1:T(8,128)(2,1)} %get-tuple-element.469, ...), kind=kOutput, calls=%fused_computation.19.clone.1 | convolution fusion | flops 557840384 | bytes 35930116 | tf_op jit(solution)/shard_map/while/body/eval_jaxpr/qhd,khd->hqk/dot_general | solution.py:118
  181.3 11.0 %multiply_convert_fusion.5 = bf16[4,512,2048]{2,1,0:T(8,128)(2,1)} fusion(f32[4,512,2048]{2,1,0:T(8,128)} %get-tuple-element.383, f32[4,512,2048]{2,1,0:T(8,128)S(1)} %bitcast.210, f32[4,512]{1,0:T(4,128)} %get-tuple-element.384, f32[4,512]{1,0:T(4,128)S(1)} %dynamic-slice_bitcast_fusion.2, pred[512,2048]{1,0:T(8,128)(4,1)} %fusion.161), kind=kLoop, calls=%fused_computation.18.clone.1 | loop fusion | flops 25165824 | bytes 43008000 | tf_op jit(solution)/shard_map/while/body/eval_jaxpr/convert_element_type | solution.py:121
  199.1 11.1 %dynamic_update_slice.20 = f32[4,512,4,64]{1,0,3,2:T(4,128)} dynamic-update-slice(f32[4,512,4,64]{1,0,3,2:T(4,128)} %get-tuple-element.444, f32[1,512,4,64]{1,0,3,2:T(1,128)S(1)} %copy.49, s32[]{:T(128)} %get-tuple-element.441, s32[]{:T(128)} %constant.52.clone.1..sunk.1, s32[]{:T(128)} %constant.52.clone.1..sunk.1, s32[]{:T(128)} %constant.52.clone.1..sunk.1) | dynamic-update-slice | bytes 1048580 | tf_op jit(solution)/shard_map/while/body/jit(dynamic_update_index_in_dim)/dynamic_update_slice | solution.py:140
  216.6 11.9 %fusion.163 = f32[2048,4,64]{0,2,1:T(8,128)} fusion(f32[4,512,2048]{2,1,0:T(8,128)} %fusion.160, f32[4,512]{1,0:T(4,128)S(1)} %dynamic-slice_bitcast_fusion.2, pred[512,2048]{1,0:T(8,128)(4,1)S(1)} %copy-done.3, f32[2048,4,64]{0,2,1:T(8,128)} %get-tuple-element.443, pred[]{:T(512)S(6)} %compare.3, bf16[2048,4,64]{0,2,1:T(8,128)(2,1)} %get-tuple-element.468, ...), kind=kOutput, calls=%fused_computation.30.clone.1 | convolution fusion | flops 554696704 | bytes 22290436 | tf_op jit(solution)/shard_map/while/body/eval_jaxpr/hqk,qhd->khd/dot_general | solution.py:131
  232.0 9.1 fusion.160
  243.8 15.8 %multiply_reduce_fusion.2 = (f32[4,512]{1,0:T(4,128)}, f32[4,512,2048]{2,1,0:T(8,128)}) fusion(f32[4,512,2048]{2,1,0:T(8,128)} %fusion.160, f32[4,512]{1,0:T(4,128)S(1)} %dynamic-slice_bitcast_fusion.2, pred[512,2048]{1,0:T(8,128)(4,1)} %fusion.161, bf16[2048,4,64]{0,2,1:T(8,128)(2,1)} %get-tuple-element.469, ...), kind=kOutput, calls=%fused_computation.19.clone.1 | convolution fusion | flops 557840384 | bytes 35930116 | tf_op jit(solution)/shard_map/while/body/eval_jaxpr/qhd,khd->hqk/dot_general | solution.py:118
  260.9 11.0 %multiply_convert_fusion.5 = bf16[4,512,2048]{2,1,0:T(8,128)(2,1)} fusion(f32[4,512,2048]{2,1,0:T(8,128)} %get-tuple-element.383, f32[4,512,2048]{2,1,0:T(8,128)S(1)} %bitcast.210, f32[4,512]{1,0:T(4,128)} %get-tuple-element.384, f32[4,512]{1,0:T(4,128)S(1)} %dynamic-slice_bitcast_fusion.2, pred[512,2048]{1,0:T(8,128)(4,1)} %fusion.161), kind=kLoop, calls=%fused_computation.18.clone.1 | loop fusion | flops 25165824 | bytes 43008000 | tf_op jit(solution)/shard_map/while/body/eval_jaxpr/convert_element_type | solution.py:121
  278.7 11.1 %dynamic_update_slice.20 = f32[4,512,4,64]{1,0,3,2:T(4,128)} dynamic-update-slice(f32[4,512,4,64]{1,0,3,2:T(4,128)} %get-tuple-element.444, f32[1,512,4,64]{1,0,3,2:T(1,128)S(1)} %copy.49, s32[]{:T(128)} %get-tuple-element.441, s32[]{:T(128)} %constant.52.clone.1..sunk.1, s32[]{:T(128)} %constant.52.clone.1..sunk.1, s32[]{:T(128)} %constant.52.clone.1..sunk.1) | dynamic-update-slice | bytes 1048580 | tf_op jit(solution)/shard_map/while/body/jit(dynamic_update_index_in_dim)/dynamic_update_slice | solution.py:140
  296.8 12.5 %fusion.163 = f32[2048,4,64]{0,2,1:T(8,128)} fusion(f32[4,512,2048]{2,1,0:T(8,128)} %fusion.160, f32[4,512]{1,0:T(4,128)S(1)} %dynamic-slice_bitcast_fusion.2, pred[512,2048]{1,0:T(8,128)(4,1)S(1)} %copy-done.3, f32[2048,4,64]{0,2,1:T(8,128)} %get-tuple-element.443, pred[]{:T(512)S(6)} %compare.3, bf16[2048,4,64]{0,2,1:T(8,128)(2,1)} %get-tuple-element.468, ...), kind=kOutput, calls=%fused_computation.30.clone.1 | convolution fusion | flops 554696704 | bytes 22290436 | tf_op jit(solution)/shard_map/while/body/eval_jaxpr/hqk,qhd->khd/dot_general | solution.py:131
  312.9 9.1 fusion.160
  324.6 15.8 %multiply_reduce_fusion.2 = (f32[4,512]{1,0:T(4,128)}, f32[4,512,2048]{2,1,0:T(8,128)}) fusion(f32[4,512,2048]{2,1,0:T(8,128)} %fusion.160, f32[4,512]{1,0:T(4,128)S(1)} %dynamic-slice_bitcast_fusion.2, pred[512,2048]{1,0:T(8,128)(4,1)} %fusion.161, bf16[2048,4,64]{0,2,1:T(8,128)(2,1)} %get-tuple-element.469, ...), kind=kOutput, calls=%fused_computation.19.clone.1 | convolution fusion | flops 557840384 | bytes 35930116 | tf_op jit(solution)/shard_map/while/body/eval_jaxpr/qhd,khd->hqk/dot_general | solution.py:118
  341.7 11.0 %multiply_convert_fusion.5 = bf16[4,512,2048]{2,1,0:T(8,128)(2,1)} fusion(f32[4,512,2048]{2,1,0:T(8,128)} %get-tuple-element.383, f32[4,512,2048]{2,1,0:T(8,128)S(1)} %bitcast.210, f32[4,512]{1,0:T(4,128)} %get-tuple-element.384, f32[4,512]{1,0:T(4,128)S(1)} %dynamic-slice_bitcast_fusion.2, pred[512,2048]{1,0:T(8,128)(4,1)} %fusion.161), kind=kLoop, calls=%fused_computation.18.clone.1 | loop fusion | flops 25165824 | bytes 43008000 | tf_op jit(solution)/shard_map/while/body/eval_jaxpr/convert_element_type | solution.py:121
  359.6 11.1 %dynamic_update_slice.20 = f32[4,512,4,64]{1,0,3,2:T(4,128)} dynamic-update-slice(f32[4,512,4,64]{1,0,3,2:T(4,128)} %get-tuple-element.444, f32[1,512,4,64]{1,0,3,2:T(1,128)S(1)} %copy.49, s32[]{:T(128)} %get-tuple-element.441, s32[]{:T(128)} %constant.52.clone.1..sunk.1, s32[]{:T(128)} %constant.52.clone.1..sunk.1, s32[]{:T(128)} %constant.52.clone.1..sunk.1) | dynamic-update-slice | bytes 1048580 | tf_op jit(solution)/shard_map/while/body/jit(dynamic_update_index_in_dim)/dynamic_update_slice | solution.py:140
  377.7 12.5 %fusion.163 = f32[2048,4,64]{0,2,1:T(8,128)} fusion(f32[4,512,2048]{2,1,0:T(8,128)} %fusion.160, f32[4,512]{1,0:T(4,128)S(1)} %dynamic-slice_bitcast_fusion.2, pred[512,2048]{1,0:T(8,128)(4,1)S(1)} %copy-done.3, f32[2048,4,64]{0,2,1:T(8,128)} %get-tuple-element.443, pred[]{:T(512)S(6)} %compare.3, bf16[2048,4,64]{0,2,1:T(8,128)(2,1)} %get-tuple-element.468, ...), kind=kOutput, calls=%fused_computation.30.clone.1 | convolution fusion | flops 554696704 | bytes 22290436 | tf_op jit(solution)/shard_map/while/body/eval_jaxpr/hqk,qhd->khd/dot_general | solution.py:131
  405.5 15.8 %multiply_reduce_fusion.2 = (f32[4,512]{1,0:T(4,128)}, f32[4,512,2048]{2,1,0:T(8,128)}) fusion(f32[4,512,2048]{2,1,0:T(8,128)} %fusion.160, f32[4,512]{1,0:T(4,128)S(1)} %dynamic-slice_bitcast_fusion.2, pred[512,2048]{1,0:T(8,128)(4,1)} %fusion.161, bf16[2048,4,64]{0,2,1:T(8,128)(2,1)} %get-tuple-element.469, ...), kind=kOutput, calls=%fused_computation.19.clone.1 | convolution fusion | flops 557840384 | bytes 35930116 | tf_op jit(solution)/shard_map/while/body/eval_jaxpr/qhd,khd->hqk/dot_general | solution.py:118
  422.6 11.0 %multiply_convert_fusion.5 = bf16[4,512,2048]{2,1,0:T(8,128)(2,1)} fusion(f32[4,512,2048]{2,1,0:T(8,128)} %get-tuple-element.383, f32[4,512,2048]{2,1,0:T(8,128)S(1)} %bitcast.210, f32[4,512]{1,0:T(4,128)} %get-tuple-element.384, f32[4,512]{1,0:T(4,128)S(1)} %dynamic-slice_bitcast_fusion.2, pred[512,2048]{1,0:T(8,128)(4,1)} %fusion.161), kind=kLoop, calls=%fused_computation.18.clone.1 | loop fusion | flops 25165824 | bytes 43008000 | tf_op jit(solution)/shard_map/while/body/eval_jaxpr/convert_element_type | solution.py:121
  440.4 11.1 %dynamic_update_slice.20 = f32[4,512,4,64]{1,0,3,2:T(4,128)} dynamic-update-slice(f32[4,512,4,64]{1,0,3,2:T(4,128)} %get-tuple-element.444, f32[1,512,4,64]{1,0,3,2:T(1,128)S(1)} %copy.49, s32[]{:T(128)} %get-tuple-element.441, s32[]{:T(128)} %constant.52.clone.1..sunk.1, s32[]{:T(128)} %constant.52.clone.1..sunk.1, s32[]{:T(128)} %constant.52.clone.1..sunk.1) | dynamic-update-slice | bytes 1048580 | tf_op jit(solution)/shard_map/while/body/jit(dynamic_update_index_in_dim)/dynamic_update_slice | solution.py:140
  458.5 12.5 %fusion.163 = f32[2048,4,64]{0,2,1:T(8,128)} fusion(f32[4,512,2048]{2,1,0:T(8,128)} %fusion.160, f32[4,512]{1,0:T(4,128)S(1)} %dynamic-slice_bitcast_fusion.2, pred[512,2048]{1,0:T(8,128)(4,1)S(1)} %copy-done.3, f32[2048,4,64]{0,2,1:T(8,128)} %get-tuple-element.443, pred[]{:T(512)S(6)} %compare.3, bf16[2048,4,64]{0,2,1:T(8,128)(2,1)} %get-tuple-element.468, ...), kind=kOutput, calls=%fused_computation.30.clone.1 | convolution fusion | flops 554696704 | bytes 22290436 | tf_op jit(solution)/shard_map/while/body/eval_jaxpr/hqk,qhd->khd/dot_general | solution.py:131
  490.2 14.7 %fusion.98 = f32[2048,1024]{1,0:T(8,128)} fusion(bf16[2048,1024]{1,0:T(8,128)(2,1)} %param.25, bf16[1,2048,2048]{2,1,0:T(8,128)(2,1)} %param.17, f32[2048]{0:T(1024)S(1)} %copy-done.23, f32[2048]{0:T(1024)S(1)} %copy-done.21, f32[2048]{0:T(1024)S(1)} %copy-done.19, f32[2048]{0:T(1024)S(1)} %copy-done.17), kind=kOutput, calls=%fused_computation.146 | convolution fusion | flops 8615100416 | bytes 21004288 | tf_op jit(solution)/shard_map/dot_general | solution.py:182
  504.9 10.4 %fusion.102 = f32[2048,2048]{1,0:T(8,128)} fusion(bf16[2048,768]{0,1:T(8,128)(2,1)S(1)} %bitcast.222, bf16[2048,768]{0,1:T(8,128)(2,1)S(1)} %bitcast.220), kind=kOutput, calls=%fused_computation.149 | convolution fusion | flops 6442450944 | bytes 23068672 | tf_op jit(solution)/shard_map/dot_general | solution.py:50
  515.4 15.7 %fusion.96 = f32[2048,2048]{1,0:T(8,128)} fusion(bf16[1024,2048]{1,0:T(8,128)(2,1)S(1)} %copy-done.32, f32[2048,1024]{1,0:T(8,128)} %fusion.98, f32[1024]{0:T(1024)S(1)} %convert_element_type.171), kind=kOutput, calls=%fused_computation.145 | convolution fusion | flops 8610906112 | bytes 29364224 | tf_op jit(solution)/shard_map/dot_general | solution.py:186
  531.1 11.7 %add_convert_fusion.1 = bf16[2048,2048]{1,0:T(8,128)(2,1)} fusion(f32[2048,2048]{1,0:T(8,128)} %fusion.96, bf16[2048,256]{0,1:T(8,128)(2,1)S(1)} %bitcast.219, bf16[256,2048]{1,0:T(8,128)(2,1)S(1)} %copy-done), kind=kOutput, calls=%fused_computation.77 | convolution fusion | flops 2155872256 | bytes 27262976 | tf_op jit(solution)/shard_map/dot_general | solution.py:186
  542.8 18.1 %fusion.101 = (bf16[1024]{0:T(1024)(128)(2,1)S(1)}, bf16[2048,1024]{1,0:T(8,128)(2,1)}) fusion(f32[2048,1024]{1,0:T(8,128)} %fusion.98, f32[1024]{0:T(1024)S(1)} %convert_element_type.171, bf16[1024,2048]{1,0:T(8,128)(2,1)} %param.27, bf16[1,2048,2048]{2,1,0:T(8,128)(2,1)S(1)} %bitcast.212), kind=kOutput, calls=%fused_computation.148 | convolution fusion | flops 8636070912 | bytes 25171968 | tf_op jit(solution)/shard_map/dot_general | solution.py:50
  560.9 16.4 %add_convert_fusion = bf16[2048,2048]{1,0:T(8,128)(2,1)} fusion(f32[2048,2048]{1,0:T(8,128)} %fusion.102, bf16[2048,1024]{1,0:T(8,128)(2,1)} %get-tuple-element.246, bf16[2048,1024]{1,0:T(8,128)(2,1)} %param.25), kind=kOutput, calls=%fused_computation.76 | convolution fusion | flops 8598323200 | bytes 33554432 | tf_op jit(solution)/shard_map/dot_general | solution.py:50
  577.4 15.5 %convolution_convert_fusion = bf16[2048,1024]{1,0:T(8,128)(2,1)} fusion(bf16[2048,1024]{1,0:T(8,128)(2,1)} %get-tuple-element.246, bf16[1,2048,2048]{2,1,0:T(8,128)(2,1)} %param.17, f32[2048]{0:T(1024)S(1)} %copy-done.23, f32[2048]{0:T(1024)S(1)} %copy-done.21, f32[2048]{0:T(1024)S(1)} %copy-done.19, f32[2048]{0:T(1024)S(1)} %copy-done.17), kind=kOutput, calls=%fused_computation.101 | convolution fusion | flops 8617197568 | bytes 16809984 | tf_op jit(solution)/shard_map/dot_general | solution.py:44
  593.0 16.6 %fusion.80 = bf16[1024,2048]{1,0:T(8,128)(2,1)} fusion(bf16[1,2048,2048]{2,1,0:T(8,128)(2,1)} %param.29, f32[2048,1024]{1,0:T(8,128)} %fusion.98, f32[1024]{0:T(1024)S(1)} %convert_element_type.171), kind=kOutput, calls=%fused_computation.100 | convolution fusion | flops 8613003264 | bytes 20975616 | tf_op jit(solution)/shard_map/dot_general | solution.py:44
  621.0 290.9 %all-reduce.9.cloned.1.call-done = (bf16[2048,2048]{1,0:T(8,128)(2,1)}, bf16[2048,2048]{1,0:T(8,128)(2,1)}) async-done(((bf16[2048,2048]{1,0:T(8,128)(2,1)}, bf16[2048,2048]{1,0:T(8,128)(2,1)}), (bf16[2048,2048]{1,0:T(8,128)(2,1)}, bf16[2048,2048]{1,0:T(8,128)(2,1)})) %all-reduce.9.cloned.1.call-update) | async-done | bytes 16777232 | tf_op jit(solution)/shard_map/psum | solution.py:190
  916.6 10.2 %fusion.55 = (bf16[2048]{0:T(1024)(128)(2,1)S(1)}, f32[2048]{0:T(1024)S(1)}, f32[2048]{0:T(1024)S(1)}) fusion(bf16[1,2048,2048]{2,1,0:T(8,128)(2,1)} %param.17, bf16[2048,2048]{1,0:T(8,128)(2,1)} %get-tuple-element.214, f32[2048]{0:T(1024)S(1)} %copy-done.19, f32[2048]{0:T(1024)S(1)} %copy-done.17, f32[2048]{0:T(1024)S(1)} %copy-done.21), kind=kLoop, calls=%fused_computation.69 | loop fusion | flops 41936896 | bytes 16822272 | tf_op jit(solution)/shard_map/reduce_sum | solution.py:219
  926.9 12.1 %all-reduce.6 = (bf16[2048]{0:T(1024)(128)(2,1)S(1)}, bf16[2048]{0:T(1024)(128)(2,1)S(1)}, bf16[3,4,64]{2,1,0:T(4,128)(2,1)S(1)}, bf16[2048]{0:T(1024)(128)(2,1)S(1)}, bf16[16,64]{1,0:T(8,128)(2,1)S(1)}) all-reduce(bf16[2048]{0:T(1024)(128)(2,1)S(1)} %get-tuple-element.168, ...), channel_id=2, replica_groups=mesh['dp'=4,'tensor'=8] {'dp'}, use_global_device_ids=true, to_apply=%region_16.17.clone | all-reduce | flops 7936 | bytes 31744
  944.5 19.4 %fusion.71 = (bf16[1,2048,2048]{2,1,0:T(8,128)(2,1)}, bf16[1,2048,2048]{2,1,0:T(8,128)(2,1)}) fusion(bf16[1,2048,2048]{2,1,0:T(8,128)(2,1)} %param.17, bf16[2048,2048]{1,0:T(8,128)(2,1)} %get-tuple-element.214, bf16[1,2048,2048]{2,1,0:T(8,128)(2,1)} %param.29, f32[2048]{0:T(1024)S(1)} %broadcast_multiply_fusion, f32[2048]{0:T(1024)S(1)} %broadcast_multiply_fusion.1, ...), kind=kLoop, calls=%fused_computation.89 | loop fusion | flops 67108864 | bytes 50380800 | tf_op jit(solution)/shard_map/broadcast_in_dim | solution.py:256
  (286 shorter events, 261.1 us)
Async XLA Ops:
  8.0 123.2 %copy-start = (bf16[256,2048]{1,0:T(8,128)(2,1)S(1)}, bf16[256,2048]{1,0:T(8,128)(2,1)}, u32[]{:S(2)}) copy-start(bf16[256,2048]{1,0:T(8,128)(2,1)} %param.23) | copy-start | bytes 3145732
  8.0 608.7 %reduce-scatter.9.cloned.1.call-start = ((), (), s32[]{:S(2)}) async-start(), calls=%async_computation.5 | async-start | bytes 1310720 | tf_op jit(solution)/shard_map/reduce_scatter | solution.py:222
  131.1 487.4 %reduce-scatter.7.cloned.1.call-start = ((), (), s32[]{:S(2)}) async-start(), calls=%async_computation.4 | async-start | bytes 3932160 | tf_op jit(solution)/shard_map/reduce_scatter | solution.py:237
  164.1 15.8 %slice-start = ((s8[16777216]{0:T(1024)(128)(4,1)}), s8[4194304]{0:T(1024)(128)(4,1)S(1)}, s32[]{:S(2)}) async-start(s8[16777216]{0:T(1024)(128)(4,1)} %bitcast.209), calls=%async_computation.9 | async-start | bytes 8388608 | tf_op jit(solution)/shard_map/while
  164.1 15.8 %slice-start.1 = ((s8[16777216]{0:T(1024)(128)(4,1)}), s8[4194304]{0:T(1024)(128)(4,1)S(1)}, s32[]{:S(2)}) async-start(s8[16777216]{0:T(1024)(128)(4,1)} %bitcast.209), calls=%async_computation.10 | async-start | bytes 8388608 | tf_op jit(solution)/shard_map/while
  164.1 15.8 %slice-start.2 = ((s8[16777216]{0:T(1024)(128)(4,1)}), s8[4194304]{0:T(1024)(128)(4,1)S(1)}, s32[]{:S(2)}) async-start(s8[16777216]{0:T(1024)(128)(4,1)} %bitcast.209), calls=%async_computation.11 | async-start | bytes 8388608 | tf_op jit(solution)/shard_map/while
  164.1 17.1 %slice-start.3 = ((s8[16777216]{0:T(1024)(128)(4,1)}), s8[4194304]{0:T(1024)(128)(4,1)S(1)}, s32[]{:S(2)}) async-start(s8[16777216]{0:T(1024)(128)(4,1)} %bitcast.209), calls=%async_computation.12 | async-start | bytes 8388608 | tf_op jit(solution)/shard_map/while
  198.5 18.0 %copy-start.3 = (pred[512,2048]{1,0:T(8,128)(4,1)S(1)}, pred[512,2048]{1,0:T(8,128)(4,1)}, u32[]{:S(2)}) copy-start(pred[512,2048]{1,0:T(8,128)(4,1)} %fusion.161) | copy-start | bytes 3145732 | tf_op jit(solution)/shard_map/while
  243.8 15.8 %slice-start = ((s8[16777216]{0:T(1024)(128)(4,1)}), s8[4194304]{0:T(1024)(128)(4,1)S(1)}, s32[]{:S(2)}) async-start(s8[16777216]{0:T(1024)(128)(4,1)} %bitcast.209), calls=%async_computation.9 | async-start | bytes 8388608 | tf_op jit(solution)/shard_map/while
  243.8 15.8 %slice-start.1 = ((s8[16777216]{0:T(1024)(128)(4,1)}), s8[4194304]{0:T(1024)(128)(4,1)S(1)}, s32[]{:S(2)}) async-start(s8[16777216]{0:T(1024)(128)(4,1)} %bitcast.209), calls=%async_computation.10 | async-start | bytes 8388608 | tf_op jit(solution)/shard_map/while
  243.8 15.8 %slice-start.2 = ((s8[16777216]{0:T(1024)(128)(4,1)}), s8[4194304]{0:T(1024)(128)(4,1)S(1)}, s32[]{:S(2)}) async-start(s8[16777216]{0:T(1024)(128)(4,1)} %bitcast.209), calls=%async_computation.11 | async-start | bytes 8388608 | tf_op jit(solution)/shard_map/while
  243.8 17.1 %slice-start.3 = ((s8[16777216]{0:T(1024)(128)(4,1)}), s8[4194304]{0:T(1024)(128)(4,1)S(1)}, s32[]{:S(2)}) async-start(s8[16777216]{0:T(1024)(128)(4,1)} %bitcast.209), calls=%async_computation.12 | async-start | bytes 8388608 | tf_op jit(solution)/shard_map/while
  278.2 18.6 %copy-start.3 = (pred[512,2048]{1,0:T(8,128)(4,1)S(1)}, pred[512,2048]{1,0:T(8,128)(4,1)}, u32[]{:S(2)}) copy-start(pred[512,2048]{1,0:T(8,128)(4,1)} %fusion.161) | copy-start | bytes 3145732 | tf_op jit(solution)/shard_map/while
  324.6 15.8 %slice-start = ((s8[16777216]{0:T(1024)(128)(4,1)}), s8[4194304]{0:T(1024)(128)(4,1)S(1)}, s32[]{:S(2)}) async-start(s8[16777216]{0:T(1024)(128)(4,1)} %bitcast.209), calls=%async_computation.9 | async-start | bytes 8388608 | tf_op jit(solution)/shard_map/while
  324.6 15.8 %slice-start.1 = ((s8[16777216]{0:T(1024)(128)(4,1)}), s8[4194304]{0:T(1024)(128)(4,1)S(1)}, s32[]{:S(2)}) async-start(s8[16777216]{0:T(1024)(128)(4,1)} %bitcast.209), calls=%async_computation.10 | async-start | bytes 8388608 | tf_op jit(solution)/shard_map/while
  324.6 15.8 %slice-start.2 = ((s8[16777216]{0:T(1024)(128)(4,1)}), s8[4194304]{0:T(1024)(128)(4,1)S(1)}, s32[]{:S(2)}) async-start(s8[16777216]{0:T(1024)(128)(4,1)} %bitcast.209), calls=%async_computation.11 | async-start | bytes 8388608 | tf_op jit(solution)/shard_map/while
  324.6 17.1 %slice-start.3 = ((s8[16777216]{0:T(1024)(128)(4,1)}), s8[4194304]{0:T(1024)(128)(4,1)S(1)}, s32[]{:S(2)}) async-start(s8[16777216]{0:T(1024)(128)(4,1)} %bitcast.209), calls=%async_computation.12 | async-start | bytes 8388608 | tf_op jit(solution)/shard_map/while
  359.0 18.6 %copy-start.3 = (pred[512,2048]{1,0:T(8,128)(4,1)S(1)}, pred[512,2048]{1,0:T(8,128)(4,1)}, u32[]{:S(2)}) copy-start(pred[512,2048]{1,0:T(8,128)(4,1)} %fusion.161) | copy-start | bytes 3145732 | tf_op jit(solution)/shard_map/while
  405.4 15.8 %slice-start = ((s8[16777216]{0:T(1024)(128)(4,1)}), s8[4194304]{0:T(1024)(128)(4,1)S(1)}, s32[]{:S(2)}) async-start(s8[16777216]{0:T(1024)(128)(4,1)} %bitcast.209), calls=%async_computation.9 | async-start | bytes 8388608 | tf_op jit(solution)/shard_map/while
  405.4 15.8 %slice-start.1 = ((s8[16777216]{0:T(1024)(128)(4,1)}), s8[4194304]{0:T(1024)(128)(4,1)S(1)}, s32[]{:S(2)}) async-start(s8[16777216]{0:T(1024)(128)(4,1)} %bitcast.209), calls=%async_computation.10 | async-start | bytes 8388608 | tf_op jit(solution)/shard_map/while
  405.4 15.8 %slice-start.2 = ((s8[16777216]{0:T(1024)(128)(4,1)}), s8[4194304]{0:T(1024)(128)(4,1)S(1)}, s32[]{:S(2)}) async-start(s8[16777216]{0:T(1024)(128)(4,1)} %bitcast.209), calls=%async_computation.11 | async-start | bytes 8388608 | tf_op jit(solution)/shard_map/while
  405.4 17.1 %slice-start.3 = ((s8[16777216]{0:T(1024)(128)(4,1)}), s8[4194304]{0:T(1024)(128)(4,1)S(1)}, s32[]{:S(2)}) async-start(s8[16777216]{0:T(1024)(128)(4,1)} %bitcast.209), calls=%async_computation.12 | async-start | bytes 8388608 | tf_op jit(solution)/shard_map/while
  439.9 18.6 %copy-start.3 = (pred[512,2048]{1,0:T(8,128)(4,1)S(1)}, pred[512,2048]{1,0:T(8,128)(4,1)}, u32[]{:S(2)}) copy-start(pred[512,2048]{1,0:T(8,128)(4,1)} %fusion.161) | copy-start | bytes 3145732 | tf_op jit(solution)/shard_map/while
  490.0 14.9 %copy-start.31 = (bf16[1024]{0:T(1024)(128)(2,1)S(1)}, bf16[1024]{0:T(1024)(128)(2,1)}, u32[]{:S(2)}) copy-start(bf16[1024]{0:T(1024)(128)(2,1)} %param.26) | copy-start | bytes 6148
  490.0 421.8 %all-reduce.9.cloned.1.call-start = ((), (), s32[]{:S(2)}) async-start(), calls=%async_computation.8 | async-start | bytes 33554432 | tf_op jit(solution)/shard_map/psum | solution.py:190
  490.1 14.8 %copy-start.9 = (bf16[2048,3,256]{0,2,1:T(8,128)(2,1)S(1)}, bf16[2048,3,256]{0,2,1:T(8,128)(2,1)}, u32[]{:S(2)}) copy-start(bf16[2048,3,256]{0,2,1:T(8,128)(2,1)} %copy.30) | copy-start | bytes 9437188
  504.9 37.9 %slice-start.4 = ((s8[8388608]{0:T(1024)(128)(4,1)}), s8[4194304]{0:T(1024)(128)(4,1)S(1)}, s32[]{:S(2)}) async-start(s8[8388608]{0:T(1024)(128)(4,1)} %bitcast.211), calls=%async_computation.13 | async-start | bytes 8388608
  515.4 15.7 %copy-start.7 = (bf16[32,8,4,512]{3,1,2,0:T(8,128)(2,1)S(1)}, bf16[32,8,4,512]{3,1,2,0:T(8,128)(2,1)}, u32[]{:S(2)}) copy-start(bf16[32,8,4,512]{3,1,2,0:T(8,128)(2,1)} %copy-done.6) | copy-start | bytes 3145732
  515.4 27.5 %slice-start.5 = ((s8[8388608]{0:T(1024)(128)(4,1)}), s8[4194304]{0:T(1024)(128)(4,1)S(1)}, s32[]{:S(2)}) async-start(s8[8388608]{0:T(1024)(128)(4,1)} %bitcast.211), calls=%async_computation.14 | async-start | bytes 8388608
  577.4 361.7 %reduce-scatter.11.cloned.1.call-start = ((), (), s32[]{:S(2)}) async-start(), calls=%async_computation.6 | async-start | bytes 5242880 | tf_op jit(solution)/shard_map/reduce_scatter | solution.py:228
  592.9 371.0 %reduce-scatter.13.cloned.1.call-start = ((), (), s32[]{:S(2)}) async-start(), calls=%async_computation.7 | async-start | bytes 5242880 | tf_op jit(solution)/shard_map/reduce_scatter | solution.py:234
  939.1 27.7 %copy-start.25 = (f32[512]{0:T(512)}, f32[512]{0:T(512)S(1)}, u32[]{:S(2)}) copy-start(f32[512]{0:T(512)S(1)} %dynamic-slice_convert_fusion.2) | copy-start | bytes 6148
  (42 other events, 396.5 us)
Sparse Core Ops, SparseCore 0:
  131.3 28.8 reduce-scatter.8
  490.2 45.0 reduce-scatter.6
  593.0 53.8 reduce-scatter.10
  649.8 52.6 reduce-scatter.12
Sparse Core Ops, SparseCore 1:
  577.5 334.3 all-reduce.8
where the time goes:
time: 992 us; the launch traced here: 975 us
  matrix products  393 us (40%)
  waiting for transfers between devices  291 us (29%)
  other arithmetic  153 us (15%)
  local copies, waits for them, and re-layouts  83.2 us (8%)
  loops' own time  24.8 us (2%)
  between operations  18.2 us (2%)
  blocking collectives  12.1 us (1%)
    psum x1, waiting for transfers between devices, on_device(): lax.psum(partial_sum.astype(jnp.bfloat16), 'tensor').astype(jnp.float32)  291 us
    dot_general x4, matrix products, one_block(): jnp.einsum('qhd,khd->hqk', do_block, values, preferred_element_type=jnp.f...  63.2 us
    dot_general x8, matrix products, one_block(): jnp.einsum('qhd,khd->hqk', q_block, keys, preferred_element_type=jnp.floa...  54 us
    dot_general x4, matrix products, times_transposed(): lax.dot_general(left, right, (((1,), (1,)), ((), ())), preferred_element_...  51.7 us
    dot_general x4, matrix products, one_block(): jnp.einsum('hqk,qhd->khd', probability.astype(jnp.bfloat16), do_block, pr...  49.3 us
    dot_general x4, matrix products, contract_rows(): lax.dot_general(left, right, (((0,), (0,)), ((), ())), preferred_element_...  47.1 us
    dynamic_update_slice x8, local copies, waits for them, and re-layouts, attention_backward(): lax.scan(one_block, (empty, empty), jnp.arange(length // block_rows))  46.6 us
    convert_element_type x4, other arithmetic, one_block(): grad_scores = (probability * (grad_prob - jnp.sum(probability * grad_prob...  44 us
  transfers between devices with their start and end apart: 5, of which 1 were waited for; matrix products, arithmetic and copies ran while one was open for 51% of the time, Pallas kernels for 0%

commit v1 on v0

v1 whole, which is shorter than its diff:
```python
from functools import partial

import jax
import jax.numpy as jnp
from jax import lax
from jax.experimental import pallas as pl
from jax.experimental.pallas import tpu as pltpu
from jax.sharding import PartitionSpec as P

HD = 64
ROT = 32
PAIR = 2 * HD
TILE = 256
CHUNKS = 4
NEG = -1e30
MIB = 1 << 20
F32 = jnp.float32
BF16 = jnp.bfloat16


class Chain:
    def __init__(self):
        self.link = jnp.zeros((8, 128), F32)

    def __call__(
        self, kernel, name, grid, ins, outs, scalars=(), scratch=(), alias=(), flops=0.0, moved=0.0, mib=58
    ):
        taken, given = len(scalars) + len(ins), len(outs)

        def body(*refs):
            kernel(*refs[:taken], *refs[taken + 1 : taken + 1 + given], *refs[taken + 2 + given :])

        anywhere = pl.BlockSpec(memory_space=pl.ANY)
        results = pl.pallas_call(
            body,
            grid_spec=pltpu.PrefetchScalarGridSpec(
                num_scalar_prefetch=len(scalars),
                grid=(grid,),
                in_specs=[spec for _, spec in ins] + [anywhere],
                out_specs=[spec for _, _, spec in outs] + [anywhere],
                scratch_shapes=list(scratch),
            ),
            out_shape=[jax.ShapeDtypeStruct(shape, dtype) for shape, dtype, _ in outs]
            + [jax.ShapeDtypeStruct(self.link.shape, F32)],
            input_output_aliases={taken: given, **{len(scalars) + i: o for i, o in alias}},
            compiler_params=pltpu.CompilerParams(
                dimension_semantics=("arbitrary",), vmem_limit_bytes=mib * MIB
            ),
            cost_estimate=pl.CostEstimate(
                flops=int(flops), bytes_accessed=int(moved), transcendentals=0
            ),
            name=name,
        )(*scalars, *[array for array, _ in ins], self.link)
        self.link = results[-1]
        return results[:-1]


def whole(shape):
    zeros = (0,) * len(shape)
    return pl.BlockSpec(shape, lambda *i: zeros)


def rows(n, height=TILE):
    return pl.BlockSpec((height, n), lambda i, *s: (i, 0))


def nn(a, b):
    return lax.dot_general(a, b, (((1,), (0,)), ((), ())), preferred_element_type=F32)


def nt(a, b):
    return lax.dot_general(a, b, (((1,), (1,)), ((), ())), preferred_element_type=F32)


def tn(a, b):
    return lax.dot_general(a, b, (((0,), (0,)), ((), ())), preferred_element_type=F32)


def column(row, width):
    return jnp.broadcast_to(row, (width, row.shape[1])).T


def rotated(x, cos_wide, sin_wide):
    lane = lax.broadcasted_iota(jnp.int32, x.shape, 1) % HD
    half = ROT // 2
    other = jnp.where(
        lane < half, pltpu.roll(x, PAIR - half, 1), pltpu.roll(x, half, 1)
    )
    return x * cos_wide + other * sin_wide


def row_stats(x):
    mean = jnp.mean(x, axis=-1, keepdims=True)
    centered = x - mean
    inverse = lax.rsqrt(jnp.mean(centered * centered, axis=-1, keepdims=True) + 1e-05)
    return centered * inverse, mean, inverse


def gelu_both(u):
    c = 0.7978845608028654
    u2 = u * u
    gate = 0.5 + 0.5 * jnp.tanh(u * (c + (c * 0.044715) * u2))
    value = u * gate
    slope = gate + value * (1.0 - gate) * (2.0 * c + (6.0 * c * 0.044715) * u2)
    return value, slope


def first_kernel(
    x0_ref, x1_ref, x2_ref, small_ref, wq_ref, bq_ref, wu_ref, bu_ref, start_ref, freq_ref,
    normed_ref, stats_ref, q_ref, k_ref, v_ref, hidden_ref, slope_ref, cos_ref, sin_ref,
    even, odd, even_stats,
):
    s = pl.program_id(0)
    gain, shift = small_ref[0:1], small_ref[1:2]
    lane = lax.broadcasted_iota(jnp.int32, (TILE, PAIR), 1)

    def norm(x):
        scaled, mean, inverse = row_stats(x.astype(F32))
        return (scaled * gain + shift).astype(BF16), jnp.where(lane == 0, mean, inverse)

    @pl.when(s == 0)
    def _():
        even[...], even_stats[...] = norm(x0_ref[...])

    half = ROT // 2
    unit = lax.broadcasted_iota(jnp.int32, (half, PAIR), 1) % HD
    index = lax.broadcasted_iota(jnp.int32, (half, PAIR), 0)
    first_half = (unit == index).astype(F32)
    second_half = (unit == index + half).astype(F32)
    bias = bq_ref[...].astype(F32)

    def spread(a, b):
        return lax.dot_general(
            a, b, (((0,), (0,)), ((), ())), precision=lax.Precision.HIGHEST,
            preferred_element_type=F32,
        )

    def project(t, normed):
        here = slice(t * TILE, (t + 1) * TILE)
        place = lax.broadcasted_iota(jnp.int32, (1, TILE), 1) + (2 * s + t) * TILE
        angle = freq_ref[...] * (place - start_ref[:, here]).astype(F32)
        cos_wide = spread(jnp.cos(angle), first_half + second_half)
        cos_wide = jnp.where(lane % HD < ROT, cos_wide, 1.0)
        sin_wide = spread(jnp.sin(angle), second_half - first_half)
        cos_ref[here], sin_ref[here] = cos_wide, sin_wide
        for c, out in enumerate((q_ref, k_ref, v_ref)):
            packed = nn(normed, wq_ref[c]) + bias[c : c + 1]
            if c == 2:
                out[here] = packed.astype(BF16)
            else:
                for p in range(packed.shape[1] // PAIR):
                    cut = slice(p * PAIR, (p + 1) * PAIR)
                    turned = rotated(packed[:, cut], cos_wide, sin_wide).astype(BF16)
                    out[here, cut] = turned * (HD**-0.5) if c == 0 else turned
        units = wu_ref.shape[1]
        for n in range(0, units, TILE):
            cut = slice(n, n + TILE)
            value, slope = gelu_both(nn(normed, wu_ref[:, cut]) + bu_ref[:, cut])
            hidden_ref[here, cut] = value.astype(BF16)
            slope_ref[here, cut] = slope.astype(BF16)

    normed = even[...]
    normed_ref[:TILE] = normed
    stats_ref[:TILE] = even_stats[...]
    after, after_stats = norm(x1_ref[...])
    odd[...] = after
    normed_ref[TILE:] = after
    stats_ref[TILE:] = after_stats
    project(0, normed)
    even[...], even_stats[...] = norm(x2_ref[...])
    project(1, odd[...])


def first(chain, x, small, wq, bq, wu, bu, start):
    length, d = x.shape
    width, units = wq.shape[2], wu.shape[1]
    tiles = length // TILE
    freq = 10000.0 ** (-jnp.arange(ROT // 2, dtype=F32) * 2.0 / ROT)
    at = lambda f: pl.BlockSpec((TILE, d), lambda s: (f(s), 0))
    big = lambda n: rows(n, 2 * TILE)
    return chain(
        first_kernel,
        "first",
        tiles // 2,
        [
            (x, at(lambda s: 0)),
            (x, at(lambda s: 2 * s + 1)),
            (x, at(lambda s: jnp.minimum(2 * s + 2, tiles - 1))),
            (small, whole(small.shape)), (wq, whole(wq.shape)), (bq, whole(bq.shape)),
            (wu, whole(wu.shape)), (bu[None].astype(F32), whole((1, units))),
            (start[None], pl.BlockSpec((1, 2 * TILE), lambda s: (0, s))),
            (jnp.broadcast_to(freq[:, None], (ROT // 2, TILE)), whole((ROT // 2, TILE))),
        ],
        [((length, d), BF16, big(d)), ((length, PAIR), F32, big(PAIR))]
        + [((length, n), BF16, big(n)) for n in (width, width, width, units, units)]
        + [((length, PAIR), F32, big(PAIR))] * 2,
        scratch=[pltpu.VMEM((TILE, d), BF16)] * 2 + [pltpu.VMEM((TILE, PAIR), F32)],
        flops=2 * length * d * (3 * width + units),
        moved=2 * length * d * 4,
    )


def attend_kernel(start_sref, start_ref, q_ref, k_ref, v_ref, mixed_ref, log_ref):
    i = pl.program_id(0)
    pairs = q_ref.shape[1] // PAIR
    left = lax.broadcasted_iota(jnp.int32, (TILE, PAIR), 1) < HD
    zero = jnp.zeros((TILE, PAIR), BF16)
    start = column(start_ref[...], TILE) - lax.broadcasted_iota(jnp.int32, (TILE, TILE), 1)
    ahead = lax.broadcasted_iota(jnp.int32, (TILE, TILE), 0) - lax.broadcasted_iota(
        jnp.int32, (TILE, TILE), 1
    )
    heads = []
    for p in range(pairs):
        q = q_ref[:, p * PAIR : (p + 1) * PAIR]
        heads += [jnp.where(left, q, zero), jnp.where(left, zero, q)]

    def step(j, carry):
        tops, totals, sums = carry
        base = j * TILE
        allowed = (start <= base) & (ahead >= base - i * TILE)
        new_tops, new_totals, new_sums = [], [], []
        for p in range(pairs):
            cut = slice(p * PAIR, (p + 1) * PAIR)
            k = k_ref[pl.ds(pl.multiple_of(base, TILE), TILE), cut]
            v = v_ref[pl.ds(pl.multiple_of(base, TILE), TILE), cut]
            shrink, grown = [], []
            for e in range(2):
                h = 2 * p + e
                s = jnp.where(allowed, nt(heads[h], k), NEG)
                top = jnp.maximum(tops[h], jnp.max(s, axis=1, keepdims=True))
                alpha = jnp.exp(tops[h] - top)
                w = jnp.exp(s - top)
                new_tops.append(top)
                new_totals.append(totals[h] * alpha + jnp.sum(w, axis=1, keepdims=True))
                shrink.append(alpha)
                vh = jnp.where(left, v, zero) if e == 0 else jnp.where(left, zero, v)
                grown.append(nn(w.astype(BF16), vh))
            new_sums.append(sums[p] * jnp.where(left, *shrink) + (grown[0] + grown[1]))
        return tuple(new_tops), tuple(new_totals), tuple(new_sums)

    empty = (
        tuple(jnp.full((TILE, 1), NEG, F32) for _ in range(2 * pairs)),
        tuple(jnp.zeros((TILE, 1), F32) for _ in range(2 * pairs)),
        tuple(jnp.zeros((TILE, PAIR), F32) for _ in range(pairs)),
    )
    low = start_sref[i * TILE] // TILE
    tops, totals, sums = lax.fori_loop(low, i + 1, step, empty)
    lane = lax.broadcasted_iota(jnp.int32, (TILE, PAIR), 1)
    logs = jnp.zeros((TILE, PAIR), F32)
    for p in range(pairs):
        scale = jnp.where(left, 1.0 / totals[2 * p], 1.0 / totals[2 * p + 1])
        mixed_ref[:, p * PAIR : (p + 1) * PAIR] = (sums[p] * scale).astype(BF16)
        for h in (2 * p, 2 * p + 1):
            logs = jnp.where(lane == h, tops[h] + jnp.log(totals[h]), logs)
    log_ref[...] = logs.T[:8]


def attend(chain, start, q, k, v):
    length, width = q.shape
    full = whole((length, width))
    return chain(
        attend_kernel,
        "attend",
        length // TILE,
        [
            (start[None], pl.BlockSpec((1, TILE), lambda i, *s: (0, i))),
            (q, rows(width)), (k, full), (v, full),
        ],
        [
            ((length, width), BF16, rows(width)),
            ((8, length), F32, pl.BlockSpec((8, TILE), lambda i, *s: (0, i))),
        ],
        scalars=(start,),
        flops=15e9,
        moved=8 * length * width,
    )


def attend_back_kernel(
    begin, start_sref, start_ref, log_ref, delta_ref, q_ref, k_ref, v_ref, g_ref, cos_ref, sin_ref,
    totals_in, gq_ref, gk_ref, gv_ref, bias_ref, totals,
):
    j = pl.program_id(0) + begin
    length, width = q_ref.shape
    pairs = width // PAIR
    here = pl.ds(pl.multiple_of(j * TILE, TILE), TILE)

    @pl.when(pl.program_id(0) == 0)
    def _():
        totals[...] = totals_in[...] if begin else jnp.zeros_like(totals)
        bias_ref[...] = jnp.zeros_like(bias_ref)

    left = lax.broadcasted_iota(jnp.int32, (TILE, PAIR), 1) < HD
    zero = jnp.zeros((TILE, PAIR), BF16)
    key_place = j * TILE + lax.broadcasted_iota(jnp.int32, (TILE, TILE), 0)
    ahead = lax.broadcasted_iota(jnp.int32, (TILE, TILE), 1) - lax.broadcasted_iota(
        jnp.int32, (TILE, TILE), 0
    )

    def halves(x):
        return jnp.where(left, x, zero), jnp.where(left, zero, x)

    keys = [k_ref[here, p * PAIR : (p + 1) * PAIR] for p in range(pairs)]
    split = [halves(k) for k in keys]
    values = [v_ref[here, p * PAIR : (p + 1) * PAIR] for p in range(pairs)]

    def step(i, carry):
        gks, gvs = carry
        there = pl.ds(pl.multiple_of(i * TILE, TILE), TILE)
        allowed = (key_place >= start_ref[:, there]) & (ahead >= (j - i) * TILE)
        new_gk, new_gv = [], []
        for p in range(pairs):
            cut = slice(p * PAIR, (p + 1) * PAIR)
            qs = halves(q_ref[there, cut])
            gs = halves(g_ref[there, cut])
            gk, gv = gks[p], gvs[p]
            gq = totals[there, cut]
            for e in range(2):
                h = 2 * p + e
                s = nt(keys[p], qs[e]) - log_ref[h : h + 1, there]
                w = jnp.exp(jnp.where(allowed, s, NEG))
                gp = nt(values[p], gs[e])
                ds = (w * (gp - delta_ref[h : h + 1, there])).astype(BF16)
                gv = gv + nn(w.astype(BF16), gs[e])
                gk = gk + nn(ds, qs[e])
                gq = gq + tn(ds, split[p][e])
            totals[there, cut] = gq
            new_gk.append(gk)
            new_gv.append(gv)
        return tuple(new_gk), tuple(new_gv)

    high = sum((start_sref[b * TILE] < (j + 1) * TILE).astype(jnp.int32) for b in range(length // TILE))
    empty = tuple(jnp.zeros((TILE, PAIR), F32) for _ in range(pairs))
    gks, gvs = lax.fori_loop(j, high, step, (empty, empty))
    cos_wide, sin_wide = cos_ref[...], -sin_ref[...]
    for p in range(pairs):
        cut = slice(p * PAIR, (p + 1) * PAIR)
        gq = rotated(totals[here, cut] * (HD**-0.5), cos_wide, sin_wide).astype(BF16)
        gk = rotated(gks[p], cos_wide, sin_wide).astype(BF16)
        gv = gvs[p].astype(BF16)
        for c, (g, out) in enumerate(((gq, gq_ref), (gk, gk_ref), (gv, gv_ref))):
            out[:, cut] = g
            bias_ref[c : c + 1, cut] += jnp.sum(g.astype(F32), axis=0, keepdims=True)


def attend_back(chain, begin, end, start, log, delta, q, k, v, g, cos_wide, sin_wide, before):
    length, width = q.shape
    full = whole((length, width))
    shifted = pl.BlockSpec((TILE, PAIR), lambda i, *s: (i + begin, 0))
    return chain(
        partial(attend_back_kernel, begin),
        f"attend_back_{begin}",
        end - begin,
        [
            (start[None], whole((1, length))), (log, whole((8, length))), (delta, whole((8, length))),
            (q, full), (k, full), (v, full), (g, full), (cos_wide, shifted), (sin_wide, shifted),
            (before, full if begin else pl.BlockSpec(memory_space=pl.ANY)),
        ],
        [(((end - begin) * TILE, width), BF16, rows(width))] * 3
        + [((8, width), F32, whole((8, width))), ((length, width), F32, full)],
        scalars=(start,),
        flops=17e9,
        moved=14 * length * width,
    )


def half_rows(chunks, half):
    def spec(n):
        def index(i, core):
            return (2 * (i % chunks) + jnp.where(i < chunks, 1 - core[0], core[0]), 0)

        return pl.BlockSpec((half, n), index)

    return spec


def store_part(total, parts):
    for n, part in enumerate(parts):

        @pl.when(pl.program_id(0) == n)
        def _():
            part[...] = total


def branch_kernel(core_ref, mixed_ref, hidden_ref, wo_ref, wd_ref, *parts):
    total = (nn(mixed_ref[...], wo_ref[...]) + nn(hidden_ref[...], wd_ref[...])).astype(BF16)
    store_part(total, parts)


def branch(chain, core, chunks, mixed, hidden, wo, wd):
    length, d = mixed.shape[0], wo.shape[1]
    half = length // (2 * chunks)
    spec = half_rows(chunks, half)
    return chain(
        branch_kernel,
        "branch",
        2 * chunks,
        [
            (mixed, spec(mixed.shape[1])), (hidden, spec(hidden.shape[1])),
            (wo, whole(wo.shape)), (wd, whole(wd.shape)),
        ],
        [((half, d), BF16, whole((half, d)))] * (2 * chunks),
        scalars=(core,),
        flops=2 * length * d * (wo.shape[0] + wd.shape[0]),
        moved=2 * length * d * 3,
    )


def back_kernel(g_ref, slope_ref, mixed_ref, wo_ref, wd_ref, pre_ref, gm_ref, delta_ref, sums_ref, up_ref):
    @pl.when(pl.program_id(0) == 0)
    def _():
        sums_ref[...] = jnp.zeros_like(sums_ref)
        up_ref[...] = jnp.zeros_like(up_ref)

    g = g_ref[...]
    for n in range(0, wd_ref.shape[0], TILE):
        cut = slice(n, n + TILE)
        pre = (nt(g, wd_ref[cut]) * slope_ref[:, cut].astype(F32)).astype(BF16)
        pre_ref[:, cut] = pre
        up_ref[0:1, cut] += jnp.sum(pre.astype(F32), axis=0, keepdims=True)
    gm = nt(g, wo_ref[...]).astype(BF16)
    gm_ref[...] = gm
    product = gm.astype(F32) * mixed_ref[...].astype(F32)
    coarse = product.astype(BF16)
    fine = (product - coarse.astype(F32)).astype(BF16)
    width = gm.shape[1]
    pick = (
        lax.broadcasted_iota(jnp.int32, (8, width), 1) // HD
        == lax.broadcasted_iota(jnp.int32, (8, width), 0)
    ).astype(BF16)
    delta_ref[...] = nt(pick, coarse) + nt(pick, fine)
    sums_ref[0:1] += jnp.sum(g.astype(F32), axis=0, keepdims=True)


def back(chain, g, slope, mixed, wo, wd):
    length, d = g.shape
    width, units = wo.shape[0], wd.shape[0]
    return chain(
        back_kernel,
        "back",
        length // TILE,
        [
            (g, rows(d)), (slope, rows(units)), (mixed, rows(width)),
            (wo, whole(wo.shape)), (wd, whole(wd.shape)),
        ],
        [
            ((length, units), BF16, rows(units)), ((length, width), BF16, rows(width)),
            ((8, length), F32, pl.BlockSpec((8, TILE), lambda i, *s: (0, i))),
            ((8, d), F32, whole((8, d))), ((8, units), F32, whole((8, units))),
        ],
        flops=2 * length * d * (width + units),
        moved=2 * length * d * 2,
    )


def normed_back_kernel(core_ref, gq_ref, gk_ref, gv_ref, pre_ref, x_ref, stats_ref, wq_ref, wu_ref, *outs):
    parts, sums_ref = outs[:-1], outs[-1]

    @pl.when(pl.program_id(0) == 0)
    def _():
        sums_ref[...] = jnp.zeros_like(sums_ref)

    mean, inverse = stats_ref[:, 0:1], stats_ref[:, 1:2]
    pieces = []
    for n in range(0, wu_ref.shape[0], 2 * TILE):
        cut = slice(n, n + 2 * TILE)
        total = nt(pre_ref[...], wu_ref[cut])
        for c, g in enumerate((gq_ref, gk_ref, gv_ref)):
            total = total + nt(g[...], wq_ref[c, cut])
        pieces.append(total.astype(BF16))
        scaled = (x_ref[:, cut].astype(F32) - mean) * inverse
        sums_ref[0:1, cut] += jnp.sum(total * scaled, axis=0, keepdims=True)
        sums_ref[1:2, cut] += jnp.sum(total, axis=0, keepdims=True)
    store_part(jnp.concatenate(pieces, axis=1), parts)


def normed_back(chain, core, chunks, gq, gk, gv, pre, x, stats, wq, wu):
    length, d = x.shape
    width, units = wq.shape[2], wu.shape[1]
    half = length // (2 * chunks)
    spec = half_rows(chunks, half)
    return chain(
        normed_back_kernel,
        "normed_back",
        2 * chunks,
        [(a, spec(width)) for a in (gq, gk, gv)]
        + [
            (pre, spec(units)), (x, spec(d)), (stats, spec(PAIR)),
            (wq, whole(wq.shape)), (wu, whole(wu.shape)),
        ],
        [((half, d), BF16, whole((half, d)))] * (2 * chunks) + [((8, d), F32, whole((8, d)))],
        scalars=(core,),
        flops=2 * length * d * (3 * width + units),
        moved=2 * length * d * 4,
    )


def weight_grad_kernel(counts, *refs):
    lefts, right, outs = refs[: len(counts)], refs[len(counts)], refs[len(counts) + 1 :]
    i = pl.program_id(0)
    done = 0
    for left, out, count in zip(lefts, outs, counts):

        @pl.when((i >= done) & (i < done + count))
        def _(left=left, out=out):
            out[...] = tn(left[...], right[...]).astype(BF16)

        done += count


def weight_grad(chain, name, lefts, right):
    length, d = right.shape
    counts = tuple(a.shape[1] // min(TILE, a.shape[1]) for a in lefts)
    ins, outs, done = [], [], 0
    for a, count in zip(lefts, counts):
        wide = a.shape[1] // count
        place = lambda i, done=done, count=count: jnp.clip(i - done, 0, count - 1)
        ins.append((a, pl.BlockSpec((length, wide), lambda i, f=place: (0, f(i)))))
        outs.append(((a.shape[1], d), BF16, pl.BlockSpec((wide, d), lambda i, f=place: (f(i), 0))))
        done += count
    total = sum(a.shape[1] for a in lefts)
    return chain(
        partial(weight_grad_kernel, counts),
        name,
        done,
        ins + [(right, whole(right.shape))],
        outs,
        flops=2 * length * d * total,
        moved=2 * length * (d + total),
    )


def add_kernel(a_ref, b_ref, out_ref):
    out_ref[...] = (a_ref[...].astype(F32) + b_ref[...].astype(F32)).astype(BF16)


def plus(chain, a, b):
    height, d = a.shape
    block = rows(d, height // 2)
    return chain(
        add_kernel, "plus", 2, [(a, block), (b, block)], [(a.shape, BF16, block)],
        flops=height * d, moved=6 * height * d, mib=16,
    )[0]


def choose_kernel(flag_ref, a_ref, b_ref, out_ref):
    out_ref[...] = jnp.where(flag_ref[0] > 0, b_ref[...], a_ref[...])


def choose(chain, flag, a, b):
    height, d = a.shape
    block = rows(d, height // 2)
    return chain(
        choose_kernel, "choose", 2, [(a, block), (b, block)], [(a.shape, BF16, block)],
        scalars=(flag,), flops=height * d, moved=6 * height * d, mib=16,
    )[0]


def assemble_kernel(core_ref, a_ref, b_ref, *rest):
    rest[-1][...] = jnp.where(core_ref[0] == pl.program_id(0), a_ref[...], b_ref[...])


def assemble(chain, core, chunk, length, a, b, so_far):
    height, d = a.shape
    block = whole((height, d))
    anywhere = pl.BlockSpec(memory_space=pl.ANY)
    return chain(
        assemble_kernel, "assemble", 2,
        [(a, block), (b, block)] + ([] if so_far is None else [(so_far, anywhere)]),
        [((length, d), BF16, pl.BlockSpec((height, d), lambda i, *s: (2 * chunk + i, 0)))],
        scalars=(core,), alias=() if so_far is None else ((2, 0),),
        flops=height * d, moved=6 * height * d, mib=16,
    )[0]


def close_output_kernel(core_ref, a_ref, b_ref, x_ref, small_ref, out_ref):
    total = a_ref[...].astype(F32) + b_ref[...].astype(F32)
    biases = small_ref[2:3] + small_ref[3:4]
    out_ref[...] = (x_ref[...].astype(F32) + total + biases).astype(BF16)


def close_grad_kernel(core_ref, a_ref, b_ref, x_ref, stats_ref, g_ref, small_ref, out_ref):
    u = (a_ref[...].astype(F32) + b_ref[...].astype(F32)) * small_ref[0:1]
    mean, inverse = stats_ref[:, 0:1], stats_ref[:, 1:2]
    scaled = (x_ref[...].astype(F32) - mean) * inverse
    back_u = inverse * (
        u
        - jnp.mean(u, axis=-1, keepdims=True)
        - scaled * jnp.mean(u * scaled, axis=-1, keepdims=True)
    )
    out_ref[...] = (g_ref[...].astype(F32) + back_u).astype(BF16)


def close(chain, kernel, name, core, chunk, a, b, own, small):
    height, d = a.shape
    part = height // 2
    block = rows(d, part)

    def mine(n):
        return pl.BlockSpec((part, n), lambda i, core: (2 * (2 * chunk + core[0]) + i, 0))

    return chain(
        kernel, name, 2,
        [(a, block), (b, block)] + [(o, mine(o.shape[1])) for o in own] + [(small, whole(small.shape))],
        [(a.shape, BF16, block)],
        scalars=(core,), flops=4 * height * d, moved=2 * height * d * (3 + len(own)), mib=16,
    )[0]


def swap_cores(value, size):
    return lax.ppermute(value, "tensor", [(i, i ^ 1) for i in range(size)])


def along(value, hops):
    return lax.ppermute(
        value, "tensor", [(2 * a + c, 2 * b + c) for a, b in hops for c in (0, 1)]
    )


def flow(chain, size, core, chunk, other, mine, closing, results, key, length):
    chips = size // 2
    chip = lax.axis_index("tensor") // 2
    distance = jnp.where(chip < chips // 2, chips // 2 - 1 - chip, chip - chips // 2)
    swapped = swap_cores(other, size)
    yield
    total = plus(chain, mine, swapped)
    for s in range(chips // 2 - 1):
        came = along(total, [(s, s + 1), (chips - 1 - s, chips - 2 - s)])
        yield
        total = plus(chain, total, came)
    a, b = chips // 2 - 1, chips // 2
    came = along(total, [(a, b), (b, a)])
    yield
    value = closing(chunk, total, came)
    for s in range(chips // 2 - 1):
        a, b = chips // 2 - 1 - s, chips // 2 + s
        came = along(value, [(a, a - 1), (b, b + 1)])
        yield
        value = choose(chain, (distance == s + 1).astype(jnp.int32)[None], value, came)
    peer = swap_cores(value, size)
    yield
    results[key] = assemble(chain, core, chunk, length, value, peer, results.get(key))


def on_device(
    size,
    inputs,
    segment_ids,
    norm_gain,
    norm_bias,
    qkv_weight,
    qkv_bias,
    out_weight,
    out_bias,
    up_weight,
    up_bias,
    down_weight,
    down_bias,
    cotangent,
):
    x, g, segment_row = inputs[0], cotangent[0], segment_ids[0]
    length, d = x.shape
    width, units = qkv_weight.shape[2], up_weight.shape[1]
    count = lax.axis_size("dp")
    core = (lax.axis_index("tensor") % 2).astype(jnp.int32)[None]

    start = jnp.sum((segment_row[None, :] < segment_row[:, None]).astype(jnp.int32), axis=1)
    small = jnp.stack([norm_gain, norm_bias, out_bias, down_bias] + [norm_gain] * 4).astype(F32)
    wq = qkv_weight.transpose(1, 0, 2)

    chain = Chain()
    normed, stats, q, k, v, hidden, slope, cos_wide, sin_wide = first(
        chain, x, small, wq, qkv_bias, up_weight, up_bias, start
    )
    mixed, log = attend(chain, start, q, k, v)
    parts = branch(chain, core, CHUNKS, mixed, hidden, out_weight, down_weight)

    results, flows = {}, []

    def close_output(chunk, a, b):
        return close(chain, close_output_kernel, "close_output", core, chunk, a, b, [x], small)

    def close_grad(chunk, a, b):
        return close(chain, close_grad_kernel, "close_grad", core, chunk, a, b, [x, stats, g], small)

    def launch(parts, closing, key):
        return [
            flow(chain, size, core, c, parts[c], parts[CHUNKS + c], closing, results, key, length)
            for c in range(CHUNKS)
        ]

    waiting = launch(parts, close_output, "output")
    for f in waiting:
        next(f)

    def advance():
        flows[:] = [f for f in flows if next(f, flows) is None]
        if waiting:
            f = waiting.pop(0)
            next(f)
            flows.append(f)

    def scatter(value):
        return lax.psum_scatter(value, "dp", scatter_dimension=1, tiled=True).astype(F32)

    advance()
    down_grad, out_grad = weight_grad(chain, "weight_grad_g", [hidden, mixed], g)
    down_share, out_share = scatter(down_grad), scatter(out_grad)
    advance()
    pre, gm, delta, g_sums, up_sums = back(chain, g, slope, mixed, out_weight, down_weight)
    advance()
    tiles = length // TILE
    cutoff = (3 * tiles) // 8
    args = (start, log, delta, q, k, v, gm, cos_wide, sin_wide)
    *one, one_sums, totals = attend_back(chain, 0, cutoff, *args, log)
    advance()
    *two, two_sums, _ = attend_back(chain, cutoff, tiles, *args, totals)
    advance()
    packed = [jnp.concatenate([a, b]) for a, b in zip(one, two)]
    *parts, norm_sums = normed_back(chain, core, CHUNKS, *packed, pre, x, stats, wq, up_weight)
    waiting += launch(parts, close_grad, "grad")
    for f in waiting:
        next(f)
    advance()
    up_grad, *qkv_grads = weight_grad(chain, "weight_grad_n", [pre] + packed, normed)
    up_share = scatter(up_grad).T
    qkv_share = scatter(jnp.concatenate(qkv_grads)).reshape(3, width, d // count).transpose(2, 0, 1)
    while flows:
        advance()

    hop = 1
    while hop < size:
        norm_sums = norm_sums + lax.ppermute(norm_sums, "tensor", [(i, i ^ hop) for i in range(size)])
        hop *= 2
    by_share = lambda a: a.reshape(-1, count, HD // count).swapaxes(0, 1).reshape(count, -1)
    narrow = jnp.concatenate([by_share(up_sums[0]), by_share((one_sums + two_sums)[:3])], axis=1)
    narrow = jnp.pad(narrow, ((0, 0), (0, d // count - narrow.shape[1]))).reshape(1, d)
    vectors = jnp.concatenate([g_sums[:1], narrow, norm_sums[:2], jnp.zeros((12, d), F32)])
    vectors = scatter(vectors.astype(BF16))
    up_b_share = vectors[1, : units // count].reshape(-1, HD // count)
    qkv_b_share = vectors[1, units // count : (units + 3 * width) // count].reshape(3, -1, HD // count)

    return (
        results["output"][None],
        results["grad"][None],
        vectors[2],
        vectors[3],
        qkv_share,
        qkv_b_share,
        out_share,
        vectors[0],
        up_share,
        up_b_share,
        down_share,
        vectors[0],
    )


def solution(mesh):
    placed = (
        P("dp", None, None),
        P("dp", None),
        P(),
        P(),
        P(None, None, "tensor"),
        P(None, "tensor"),
        P("tensor", None),
        P(),
        P(None, "tensor"),
        P("tensor"),
        P("tensor", None),
        P(),
        P("dp", None, None),
    )
    return jax.shard_map(
        partial(on_device, mesh.shape["tensor"]),
        mesh=mesh,
        in_specs=placed,
        out_specs=(
            P("dp", None, None),
            P("dp", None, None),
            P("dp"),
            P("dp"),
            P("dp", None, "tensor"),
            P(None, "tensor", "dp"),
            P("tensor", "dp"),
            P("dp"),
            P("dp", "tensor"),
            P("tensor", "dp"),
            P("tensor", "dp"),
            P("dp"),
        ),
        check_vma=False,
    )
```

time: 992 us -> 566 us (0.57); the launches traced: 975 us -> 561 us
  matrix products: 393 us -> 0 us
  Pallas kernels: 0 us -> 248 us
  waiting for transfers between devices: 291 us -> 149 us
  other arithmetic: 153 us -> 16.7 us
  starting transfers between devices: 0.21 us -> 80.8 us
  local copies, waits for them, and re-layouts: 83.2 us -> 51.2 us
  loops' own time: 24.8 us -> 0 us
  blocking collectives: 12.1 us -> 0 us
    dot_general x40 -> x0, matrix products: 393 us -> none  [the longest x4 63.2 us: one_block(): jnp.einsum('qhd,khd->hqk', do_block, values, preferred_element_type=jnp.f...]
    psum x1 -> x0, waiting for transfers between devices: 291 us -> none  [on_device(): lax.psum(partial_sum.astype(jnp.bfloat16), 'tensor').astype(jnp.float32)]
    pallas_call x0 -> x49, Pallas kernels: none -> 248 us  [__call__(): pl.pallas_call(body, grid_spec=pltpu.PrefetchScalarGridSpec(num_scalar_pr...]
    ppermute x0 -> x43, waiting for transfers between devices: none -> 148 us  [the longest x24 140 us: along(): lax.ppermute(value, 'tensor', [(2 * a + c, 2 * b + c) for a, b in hops fo...]
    ppermute x0 -> x43, starting transfers between devices: none -> 80.6 us  [the longest x24 55.8 us: along(): lax.ppermute(value, 'tensor', [(2 * a + c, 2 * b + c) for a, b in hops fo...]
    convert_element_type x19 -> x5, other arithmetic: 62.8 us -> 7.28 us  [the longest x3 5.36 us: scatter(): lax.psum_scatter(value, 'dp', scatter_dimension=1, tiled=True).astype(F32)]
    dynamic_update_slice x8 -> x0, local copies, waits for them, and re-layouts: 46.6 us -> none  [attention_backward(): lax.scan(one_block, (empty, empty), jnp.arange(length // block_rows))]
    reduce_sum x10 -> x1, other arithmetic: 47 us -> 3.17 us  [on_device(): jnp.sum((segment_row[None, :] < segment_row[:, None]).astype(jnp.int32),...]
  transfers between devices with their start and end apart: 5 -> 48, of which waited for: 1 -> 15; matrix products, arithmetic and copies ran while one was open for 51% -> 5% of each run, Pallas kernels for 0% -> 30%
where the time goes in v1:
time: 566 us; the launch traced here: 561 us
  Pallas kernels  248 us (44%)
  waiting for transfers between devices  149 us (26%)
  starting transfers between devices  80.8 us (14%)
  local copies, waits for them, and re-layouts  51.2 us (9%)
  other arithmetic  16.7 us (3%)
  between operations  14.8 us (3%)
    pallas_call x49, Pallas kernels, __call__(): pl.pallas_call(body, grid_spec=pltpu.PrefetchScalarGridSpec(num_scalar_pr...  248 us
    ppermute x24, waiting for transfers between devices, along(): lax.ppermute(value, 'tensor', [(2 * a + c, 2 * b + c) for a, b in hops fo...  140 us
    ppermute x24, starting transfers between devices, along(): lax.ppermute(value, 'tensor', [(2 * a + c, 2 * b + c) for a, b in hops fo...  55.8 us
    unnamed x89, local copies, waits for them, and re-layouts  33.6 us
    ppermute x16, starting transfers between devices, swap_cores(): return lax.ppermute(value, 'tensor', [(i, i ^ 1) for i in range(size)])  21 us
  transfers between devices with their start and end apart: 48, of which 15 were waited for; matrix products, arithmetic and copies ran while one was open for 5% of the time, Pallas kernels for 30%

profile of v1, /device:TPU:5, one launch (start us, length us, event | category | flops | bytes accessed | tf_op | source)
XLA Modules:
  0.0 560.9 jit_solution(14371955231069647676)
XLA Ops:
  8.5 3.2 convert_reduce_fusion.refs_0_
  16.5 31.7 %first.1 = (bf16[2048,2048]{1,0:T(8,128)(2,1)}, f32[2048,128]{1,0:T(8,128)}, bf16[2048,256]{1,0:T(8,128)(2,1)}, bf16[2048,256]{1,0:T(8,128)(2,1)}, bf16[2048,256...) custom-call(bf16[2048,2048]{1,0:T(8,128)(2,1)} %bitcast.28, ...), custom_call_target="tpu_custom_call", output_to_operand_aliasing={{9}: (10, {})} | custom-call | flops 15032385536 | bytes 33554432 | tf_op jit(solution)/shard_map/first/pallas_call | solution.py:34
  48.2 28.4 %attend.1 = (bf16[2048,256]{1,0:T(8,128)(2,1)}, f32[8,2048]{1,0:T(8,128)}, f32[8,128]{1,0:T(8,128)}) custom-call(s32[2048]{0:T(1024)} %convert_reduce_fusion.refs_0_, s32[1,2048]{1,0:T(1,128)} %bitcast.66, bf16[2048,256]{1,0:T(8,128)(2,1)} %get-tuple-element.148.refs_2_.refs_4_, ...), custom_call_target="tpu_custom_call", output_to_operand_aliasing={{2}: (5, {})} | custom-call | flops 15000000512 | bytes 4194304 | tf_op jit(solution)/shard_map/attend/pallas_call | solution.py:34
  76.6 19.6 %branch.1 = (bf16[256,2048]{1,0:T(8,128)(2,1)}, bf16[256,2048]{1,0:T(8,128)(2,1)}, bf16[256,2048]{1,0:T(8,128)(2,1)}, bf16[256,2048]{1,0:T(8,128)(2,1)}, bf16[25...) custom-call(s32[1]{0:T(128)} %bitcast.refs_0_, ...), custom_call_target="tpu_custom_call", output_to_operand_aliasing={{8}: (5, {})} | custom-call | flops 10737418240 | bytes 25165824 | tf_op jit(solution)/shard_map/branch/pallas_call | solution.py:34
  102.2 3.2 collective-permute-start.4
  106.2 17.8 %weight_grad_g.1 = (bf16[1024,2048]{1,0:T(8,128)(2,1)}, bf16[256,2048]{1,0:T(8,128)(2,1)}, f32[8,128]{1,0:T(8,128)}) custom-call(bf16[2048,1024]{1,0:T(8,128)(2,1)} %get-tuple-element.153.refs_2_.refs_0_, bf16[2048,256]{1,0:T(8,128)(2,1)} %get-tuple-element.152.refs_1_.refs_2_, bf16[2048,2048]{1,0:T(8,128)(2,1)} %bitcast.42, ...), custom_call_target="tpu_custom_call", output_to_operand_aliasing={{2}: (3, {})} | custom-call | flops 10737418240 | bytes 13631488 | tf_op jit(solution)/shard_map/weight_grad_g/pallas_call | solution.py:34
  124.0 3.6 collective-permute-done.4.refs_1_
  131.0 7.6 %collective-permute-start.5 = (bf16[256,2048]{1,0:T(8,128)(2,1)}, bf16[256,2048]{1,0:T(8,128)(2,1)}, u32[]{:S(2)}, u32[]{:S(2)}) collective-permute-start(bf16[256,2048]{1,0:T(8,128)(2,1)} %get-tuple-element.168.refs_0_), channel_id=1, source_target_pairs={{0,2},{1,3},{6,4},{7,5},{8,10},{9,11},{14,12},{15,13},{16,18},{17,... | collective-permute-start | bytes 3145736 | tf_op jit(solution)/shard_map/ppermute | solution.py:615
  140.5 18.8 %back.1 = (bf16[2048,1024]{1,0:T(8,128)(2,1)}, bf16[2048,256]{1,0:T(8,128)(2,1)}, f32[8,2048]{1,0:T(8,128)}, f32[8,2048]{1,0:T(8,128)}, f32[8,1024]{1,0:T(8,128)}, /*index=5*/f32[8,128]{1,0:T(8,128)}) custom-call(bf16[2048,2048]{1,0:T(8,128)(2,1)} %bitcast.43, bf16[2048,1024]{1,0:T(8,128)(2,1)} %get-tuple-element.170.refs_1_, ...), custom_call_target="tpu_custom_call", output_to_operand_aliasing={{5}: (5, {})} | custom-call | flops 10737418240 | bytes 16777216 | tf_op jit(solution)/shard_map/back/pallas_call | solution.py:34
  160.1 3.5 copy-done
  173.6 16.2 %attend_back_0.1 = (bf16[768,256]{1,0:T(8,128)(2,1)}, bf16[768,256]{1,0:T(8,128)(2,1)}, bf16[768,256]{1,0:T(8,128)(2,1)}, f32[8,256]{1,0:T(8,128)}, f32[2048,256]{1,0:T(8,128)}, /*index=5*/f32[8,128]{1,0:T(8,128)}) custom-call(s32[2048]{0:T(1024)} %convert_reduce_fusion.refs_0_, s32[1,2048]{1,0:T(1,128)} %bitcast.67, ...), custom_call_target="tpu_custom_call", output_to_operand_aliasing={{5}: (11, {})} | custom-call | flops 16999999488 | bytes 7340032 | tf_op jit(solution)/shard_map/attend_back_0/pallas_call | solution.py:34
  193.7 4.8 collective-permute-done.9.refs_2_
  199.9 3.4 copy-done.1
  214.8 30.0 %attend_back_3.1 = (bf16[1280,256]{1,0:T(8,128)(2,1)}, bf16[1280,256]{1,0:T(8,128)(2,1)}, bf16[1280,256]{1,0:T(8,128)(2,1)}, f32[8,256]{1,0:T(8,128)}, f32[2048,256]{1,0:T(8,128)}, /*index=5*/f32[8,128]{1,0:T(8,128)}) custom-call(s32[2048]{0:T(1024)} %convert_reduce_fusion.refs_0_, s32[1,2048]{1,0:T(1,128)} %bitcast.68, ...), custom_call_target="tpu_custom_call", output_to_operand_aliasing={{5}: (11, {})} | custom-call | flops 16999999488 | bytes 7340032 | tf_op jit(solution)/shard_map/attend_back_3/pallas_call | solution.py:34
  254.9 3.4 copy-done.2
  261.7 26.4 %normed_back.1 = (bf16[256,2048]{1,0:T(8,128)(2,1)}, bf16[256,2048]{1,0:T(8,128)(2,1)}, bf16[256,2048]{1,0:T(8,128)(2,1)}, bf16[256,2048]{1,0:T(8,128)(2,1)}, bf...) custom-call(s32[1]{0:T(128)} %bitcast.refs_0_, ...), custom_call_target="tpu_custom_call", output_to_operand_aliasing={{9}: (9, {})} | custom-call | flops 15032385536 | bytes 33554432 | tf_op jit(solution)/shard_map/normed_back/pallas_call | solution.py:34
  296.5 2.9 collective-permute-done.42
  307.3 22.7 %collective-permute-done.15.refs_2_ = bf16[256,2048]{1,0:T(8,128)(2,1)S(1)} collective-permute-done((bf16[256,2048]{1,0:T(8,128)(2,1)S(1)}, bf16[256,2048]{1,0:T(8,128)(2,1)S(1)}, u32[]{:S(2)}, u32[]{:S(2)}) %collective-permute-start.15) | collective-permute-done | bytes 1048608 | tf_op jit(solution)/shard_map/ppermute | solution.py:615
  330.2 3.4 copy-done.3
  336.0 24.3 %weight_grad_n.1 = (bf16[1024,2048]{1,0:T(8,128)(2,1)}, bf16[256,2048]{1,0:T(8,128)(2,1)}, bf16[256,2048]{1,0:T(8,128)(2,1)}, bf16[256,2048]{1,0:T(8,128)(2,1)}, f32[8,128]{1,0:T(8,128)}) custom-call(bf16[2048,1024]{1,0:T(8,128)(2,1)} %get-tuple-element.208.refs_4_.refs_0_, ...), custom_call_target="tpu_custom_call", output_to_operand_aliasing={{4}: (5, {})} | custom-call | flops 15032385536 | bytes 15728640 | tf_op jit(solution)/shard_map/weight_grad_n/pallas_call | solution.py:34
  360.2 3.2 pad_maximum_fusion
  366.0 6.2 %collective-permute-start.22 = (bf16[256,2048]{1,0:T(8,128)(2,1)}, bf16[256,2048]{1,0:T(8,128)(2,1)S(1)}, u32[]{:S(2)}, u32[]{:S(2)}) collective-permute-start(bf16[256,2048]{1,0:T(8,128)(2,1)} %copy-done.29), channel_id=1, source_target_pairs={{0,2},{1,3},{6,4},{7,5},{8,10},{9,11},{14,12},{15,13},{16,18},{17,... | collective-permute-start | bytes 3145736 | tf_op jit(solution)/shard_map/ppermute | solution.py:615
  374.0 19.7 %collective-permute-done.17.refs_2_ = bf16[256,2048]{1,0:T(8,128)(2,1)S(1)} collective-permute-done((bf16[256,2048]{1,0:T(8,128)(2,1)S(1)}, bf16[256,2048]{1,0:T(8,128)(2,1)S(1)}, u32[]{:S(2)}, u32[]{:S(2)}) %collective-permute-start.17) | collective-permute-done | bytes 1048608 | tf_op jit(solution)/shard_map/ppermute | solution.py:615
  396.5 5.5 collective-permute-start.25
  409.4 14.0 %collective-permute-done.25.refs_1_ = bf16[256,2048]{1,0:T(8,128)(2,1)S(1)} collective-permute-done((bf16[256,2048]{1,0:T(8,128)(2,1)S(1)}, bf16[256,2048]{1,0:T(8,128)(2,1)S(1)}, u32[]{:S(2)}, u32[]{:S(2)}) %collective-permute-start.25) | collective-permute-done | bytes 1048608 | tf_op jit(solution)/shard_map/ppermute | solution.py:615
  424.7 6.9 %collective-permute-start.27 = (bf16[256,2048]{1,0:T(8,128)(2,1)S(1)}, bf16[256,2048]{1,0:T(8,128)(2,1)S(1)}, u32[]{:S(2)}, u32[]{:S(2)}) collective-permute-start(bf16[256,2048]{1,0:T(8,128)(2,1)S(1)} %get-tuple-element.242.refs_0_), channel_id=1, source_target_pairs={{0,2},{1,3},{6,4},{7,5},{8,10},{9,11},{14,12},{15,13},{16,18},{17,... | collective-permute-start | bytes 3145736 | tf_op jit(solution)/shard_map/ppermute | solution.py:615
  434.0 14.6 %collective-permute-done.29.refs_2_ = bf16[256,2048]{1,0:T(8,128)(2,1)S(1)} collective-permute-done((bf16[256,2048]{1,0:T(8,128)(2,1)S(1)}, bf16[256,2048]{1,0:T(8,128)(2,1)S(1)}, u32[]{:S(2)}, u32[]{:S(2)}) %collective-permute-start.29) | collective-permute-done | bytes 1048608 | tf_op jit(solution)/shard_map/ppermute | solution.py:615
  455.2 5.3 collective-permute-start.30
  462.0 15.8 %collective-permute-done.32.refs_2_ = bf16[256,2048]{1,0:T(8,128)(2,1)S(1)} collective-permute-done((bf16[256,2048]{1,0:T(8,128)(2,1)S(1)}, bf16[256,2048]{1,0:T(8,128)(2,1)S(1)}, u32[]{:S(2)}, u32[]{:S(2)}) %collective-permute-start.32) | collective-permute-done | bytes 1048608 | tf_op jit(solution)/shard_map/ppermute | solution.py:615
  485.1 21.5 %collective-permute-done.35.refs_2_ = bf16[256,2048]{1,0:T(8,128)(2,1)S(1)} collective-permute-done((bf16[256,2048]{1,0:T(8,128)(2,1)S(1)}, bf16[256,2048]{1,0:T(8,128)(2,1)S(1)}, u32[]{:S(2)}, u32[]{:S(2)}) %collective-permute-start.35) | collective-permute-done | bytes 1048608 | tf_op jit(solution)/shard_map/ppermute | solution.py:615
  513.2 22.6 %collective-permute-done.37.refs_2_ = bf16[256,2048]{1,0:T(8,128)(2,1)S(1)} collective-permute-done((bf16[256,2048]{1,0:T(8,128)(2,1)S(1)}, bf16[256,2048]{1,0:T(8,128)(2,1)S(1)}, u32[]{:S(2)}, u32[]{:S(2)}) %collective-permute-start.37) | collective-permute-done | bytes 1048608 | tf_op jit(solution)/shard_map/ppermute | solution.py:615
  543.4 2.8 convert_element_type.39
  (250 shorter events, 133.1 us)
Async XLA Ops:
  7.2 530.9 %reduce-scatter.10.cloned.1.call-start = ((), (), s32[]{:S(2)}) async-start(), calls=%async_computation.7 | async-start | bytes 1310720 | tf_op jit(solution)/shard_map/reduce_scatter | solution.py:704
  102.2 25.3 %collective-permute-start.4 = (bf16[256,2048]{1,0:T(8,128)(2,1)S(1)}, bf16[256,2048]{1,0:T(8,128)(2,1)S(1)}, u32[]{:S(2)}, u32[]{:S(2)}) collective-permute-start(bf16[256,2048]{1,0:T(8,128)(2,1)S(1)} %get-tuple-element.164.refs_0_), channel_id=1, source_target_pairs={{0,2},{1,3},{6,4},{7,5},{8,10},{9,11},{14,12},{15,13},{16,18},{17,... | collective-permute-start | bytes 3145736 | tf_op jit(solution)/shard_map/ppermute | solution.py:615
  128.5 31.6 %collective-permute-start.6 = (bf16[256,2048]{1,0:T(8,128)(2,1)S(1)}, bf16[256,2048]{1,0:T(8,128)(2,1)S(1)}, u32[]{:S(2)}, u32[]{:S(2)}) collective-permute-start(bf16[256,2048]{1,0:T(8,128)(2,1)S(1)} %get-tuple-element.169.refs_1_), channel_id=1, source_target_pairs={{2,4},{3,5},{4,2},{5,3},{10,12},{11,13},{12,10},{13,11},{18,20},{1... | collective-permute-start | bytes 3145736 | tf_op jit(solution)/shard_map/ppermute | solution.py:615
  131.0 33.9 %collective-permute-start.5 = (bf16[256,2048]{1,0:T(8,128)(2,1)}, bf16[256,2048]{1,0:T(8,128)(2,1)}, u32[]{:S(2)}, u32[]{:S(2)}) collective-permute-start(bf16[256,2048]{1,0:T(8,128)(2,1)} %get-tuple-element.168.refs_0_), channel_id=1, source_target_pairs={{0,2},{1,3},{6,4},{7,5},{8,10},{9,11},{14,12},{15,13},{16,18},{17,... | collective-permute-start | bytes 3145736 | tf_op jit(solution)/shard_map/ppermute | solution.py:615
  138.5 28.0 %collective-permute-start.1 = (bf16[256,2048]{1,0:T(8,128)(2,1)}, bf16[256,2048]{1,0:T(8,128)(2,1)}, u32[]{:S(2)}, u32[]{:S(2)}) collective-permute-start(bf16[256,2048]{1,0:T(8,128)(2,1)} %get-tuple-element.158), channel_id=1, source_target_pairs={{0,1},{1,0},{2,3},{3,2},{4,5},{5,4},{6,7},{7,6},{8,9},{9,8},{10,11... | collective-permute-start | bytes 3145736 | tf_op jit(solution)/shard_map/ppermute | solution.py:611
  140.3 65.8 %collective-permute-start = (bf16[256,2048]{1,0:T(8,128)(2,1)}, bf16[256,2048]{1,0:T(8,128)(2,1)}, u32[]{:S(2)}, u32[]{:S(2)}) collective-permute-start(bf16[256,2048]{1,0:T(8,128)(2,1)} %get-tuple-element.156), channel_id=1, source_target_pairs={{0,1},{1,0},{2,3},{3,2},{4,5},{5,4},{6,7},{7,6},{8,9},{9,8},{10,11... | collective-permute-start | bytes 3145736 | tf_op jit(solution)/shard_map/ppermute | solution.py:611
  140.4 399.5 %reduce-scatter.6.cloned.1.call-start = ((), (), s32[]{:S(2)}) async-start(), calls=%async_computation.5 | async-start | bytes 81920 | tf_op jit(solution)/shard_map/reduce_scatter | solution.py:704
  169.3 35.2 %collective-permute-start.7 = (bf16[256,2048]{1,0:T(8,128)(2,1)}, bf16[256,2048]{1,0:T(8,128)(2,1)}, u32[]{:S(2)}, u32[]{:S(2)}) collective-permute-start(bf16[256,2048]{1,0:T(8,128)(2,1)} %get-tuple-element.175.refs_0_), channel_id=1, source_target_pairs={{0,2},{1,3},{6,4},{7,5},{8,10},{9,11},{14,12},{15,13},{16,18},{17,... | collective-permute-start | bytes 3145736 | tf_op jit(solution)/shard_map/ppermute | solution.py:615
  171.6 28.3 %collective-permute-start.8 = (bf16[256,2048]{1,0:T(8,128)(2,1)S(1)}, bf16[256,2048]{1,0:T(8,128)(2,1)S(1)}, u32[]{:S(2)}, u32[]{:S(2)}) collective-permute-start(bf16[256,2048]{1,0:T(8,128)(2,1)S(1)} %get-tuple-element.176.refs_1_), channel_id=1, source_target_pairs={{2,4},{3,5},{4,2},{5,3},{10,12},{11,13},{12,10},{13,11},{18,20},{1... | collective-permute-start | bytes 3145736 | tf_op jit(solution)/shard_map/ppermute | solution.py:615
  172.3 26.2 %collective-permute-start.9 = (bf16[256,2048]{1,0:T(8,128)(2,1)S(1)}, bf16[256,2048]{1,0:T(8,128)(2,1)S(1)}, u32[]{:S(2)}, u32[]{:S(2)}) collective-permute-start(bf16[256,2048]{1,0:T(8,128)(2,1)S(1)} %get-tuple-element.177.refs_1_), channel_id=1, source_target_pairs={{2,0},{3,1},{4,6},{5,7},{10,8},{11,9},{12,14},{13,15},{18,16},{19,... | collective-permute-start | bytes 3145736 | tf_op jit(solution)/shard_map/ppermute | solution.py:615
  208.9 50.5 %collective-permute-start.10 = (bf16[256,2048]{1,0:T(8,128)(2,1)}, bf16[256,2048]{1,0:T(8,128)(2,1)}, u32[]{:S(2)}, u32[]{:S(2)}) collective-permute-start(bf16[256,2048]{1,0:T(8,128)(2,1)} %get-tuple-element.188.refs_0_), channel_id=1, source_target_pairs={{0,2},{1,3},{6,4},{7,5},{8,10},{9,11},{14,12},{15,13},{16,18},{17,... | collective-permute-start | bytes 3145736 | tf_op jit(solution)/shard_map/ppermute | solution.py:615
  211.2 43.7 %collective-permute-start.11 = (bf16[256,2048]{1,0:T(8,128)(2,1)S(1)}, bf16[256,2048]{1,0:T(8,128)(2,1)S(1)}, u32[]{:S(2)}, u32[]{:S(2)}) collective-permute-start(bf16[256,2048]{1,0:T(8,128)(2,1)S(1)} %get-tuple-element.189.refs_1_), channel_id=1, source_target_pairs={{2,4},{3,5},{4,2},{5,3},{10,12},{11,13},{12,10},{13,11},{18,20},{1... | collective-permute-start | bytes 3145736 | tf_op jit(solution)/shard_map/ppermute | solution.py:615
  211.9 42.2 %collective-permute-start.12 = (bf16[256,2048]{1,0:T(8,128)(2,1)S(1)}, bf16[256,2048]{1,0:T(8,128)(2,1)S(1)}, u32[]{:S(2)}, u32[]{:S(2)}) collective-permute-start(bf16[256,2048]{1,0:T(8,128)(2,1)S(1)} %get-tuple-element.190.refs_1_), channel_id=1, source_target_pairs={{2,0},{3,1},{4,6},{5,7},{10,8},{11,9},{12,14},{13,15},{18,16},{19,... | collective-permute-start | bytes 3145736 | tf_op jit(solution)/shard_map/ppermute | solution.py:615
  213.2 37.5 %collective-permute-start.13 = (bf16[256,2048]{1,0:T(8,128)(2,1)S(1)}, bf16[256,2048]{1,0:T(8,128)(2,1)}, u32[]{:S(2)}, u32[]{:S(2)}) collective-permute-start(bf16[256,2048]{1,0:T(8,128)(2,1)S(1)} %get-tuple-element.191.refs_1_), channel_id=1, source_target_pairs={{0,1},{1,0},{2,3},{3,2},{4,5},{5,4},{6,7},{7,6},{8,9},{9,8},{10,11... | collective-permute-start | bytes 3145736 | tf_op jit(solution)/shard_map/ppermute | solution.py:611
  300.2 243.3 %reduce-scatter.14.cloned.1.call-start = ((), (), s32[]{:S(2)}) async-start(), calls=%async_computation.9 | async-start | bytes 5242880 | tf_op jit(solution)/shard_map/reduce_scatter | solution.py:704
  300.9 245.4 %reduce-scatter.8.cloned.1.call-start = ((), (), s32[]{:S(2)}) async-start(), calls=%async_computation.6 | async-start | bytes 3932160 | tf_op jit(solution)/shard_map/reduce_scatter | solution.py:704
  303.4 26.6 %collective-permute-start.15 = (bf16[256,2048]{1,0:T(8,128)(2,1)S(1)}, bf16[256,2048]{1,0:T(8,128)(2,1)S(1)}, u32[]{:S(2)}, u32[]{:S(2)}) collective-permute-start(bf16[256,2048]{1,0:T(8,128)(2,1)S(1)} %get-tuple-element.199.refs_1_), channel_id=1, source_target_pairs={{2,0},{3,1},{4,6},{5,7},{10,8},{11,9},{12,14},{13,15},{18,16},{19,... | collective-permute-start | bytes 3145736 | tf_op jit(solution)/shard_map/ppermute | solution.py:615
  304.6 25.5 %collective-permute-start.14 = (bf16[256,2048]{1,0:T(8,128)(2,1)S(1)}, bf16[256,2048]{1,0:T(8,128)(2,1)S(1)}, u32[]{:S(2)}, u32[]{:S(2)}) collective-permute-start(bf16[256,2048]{1,0:T(8,128)(2,1)S(1)} %get-tuple-element.198.refs_1_), channel_id=1, source_target_pairs={{2,4},{3,5},{4,2},{5,3},{10,12},{11,13},{12,10},{13,11},{18,20},{1... | collective-permute-start | bytes 3145736 | tf_op jit(solution)/shard_map/ppermute | solution.py:615
  305.4 28.7 %collective-permute-start.19 = (bf16[256,2048]{1,0:T(8,128)(2,1)}, bf16[256,2048]{1,0:T(8,128)(2,1)S(1)}, u32[]{:S(2)}, u32[]{:S(2)}) collective-permute-start(bf16[256,2048]{1,0:T(8,128)(2,1)} %get-tuple-element.219), channel_id=1, source_target_pairs={{0,1},{1,0},{2,3},{3,2},{4,5},{5,4},{6,7},{7,6},{8,9},{9,8},{10,11... | collective-permute-start | bytes 3145736 | tf_op jit(solution)/shard_map/ppermute | solution.py:611
  363.5 186.8 %reduce-scatter.12.cloned.1.call-start = ((), (), s32[]{:S(2)}) async-start(), calls=%async_computation.8 | async-start | bytes 5242880 | tf_op jit(solution)/shard_map/reduce_scatter | solution.py:704
  364.7 29.0 %collective-permute-start.17 = (bf16[256,2048]{1,0:T(8,128)(2,1)S(1)}, bf16[256,2048]{1,0:T(8,128)(2,1)S(1)}, u32[]{:S(2)}, u32[]{:S(2)}) collective-permute-start(bf16[256,2048]{1,0:T(8,128)(2,1)S(1)} %get-tuple-element.214.refs_1_), channel_id=1, source_target_pairs={{2,0},{3,1},{4,6},{5,7},{10,8},{11,9},{12,14},{13,15},{18,16},{19,... | collective-permute-start | bytes 3145736 | tf_op jit(solution)/shard_map/ppermute | solution.py:615
  366.0 29.0 %collective-permute-start.22 = (bf16[256,2048]{1,0:T(8,128)(2,1)}, bf16[256,2048]{1,0:T(8,128)(2,1)S(1)}, u32[]{:S(2)}, u32[]{:S(2)}) collective-permute-start(bf16[256,2048]{1,0:T(8,128)(2,1)} %copy-done.29), channel_id=1, source_target_pairs={{0,2},{1,3},{6,4},{7,5},{8,10},{9,11},{14,12},{15,13},{16,18},{17,... | collective-permute-start | bytes 3145736 | tf_op jit(solution)/shard_map/ppermute | solution.py:615
  396.5 26.9 %collective-permute-start.25 = (bf16[256,2048]{1,0:T(8,128)(2,1)S(1)}, bf16[256,2048]{1,0:T(8,128)(2,1)S(1)}, u32[]{:S(2)}, u32[]{:S(2)}) collective-permute-start(bf16[256,2048]{1,0:T(8,128)(2,1)S(1)} %get-tuple-element.237.refs_0_), channel_id=1, source_target_pairs={{0,2},{1,3},{6,4},{7,5},{8,10},{9,11},{14,12},{15,13},{16,18},{17,... | collective-permute-start | bytes 3145736 | tf_op jit(solution)/shard_map/ppermute | solution.py:615
  408.0 40.7 %collective-permute-start.29 = (bf16[256,2048]{1,0:T(8,128)(2,1)S(1)}, bf16[256,2048]{1,0:T(8,128)(2,1)S(1)}, u32[]{:S(2)}, u32[]{:S(2)}) collective-permute-start(bf16[256,2048]{1,0:T(8,128)(2,1)S(1)} %get-tuple-element.244.refs_1_), channel_id=1, source_target_pairs={{2,0},{3,1},{4,6},{5,7},{10,8},{11,9},{12,14},{13,15},{18,16},{19,... | collective-permute-start | bytes 3145736 | tf_op jit(solution)/shard_map/ppermute | solution.py:615
  423.7 27.2 %collective-permute-start.28 = (bf16[256,2048]{1,0:T(8,128)(2,1)S(1)}, bf16[256,2048]{1,0:T(8,128)(2,1)S(1)}, u32[]{:S(2)}, u32[]{:S(2)}) collective-permute-start(bf16[256,2048]{1,0:T(8,128)(2,1)S(1)} %get-tuple-element.243.refs_1_), channel_id=1, source_target_pairs={{2,4},{3,5},{4,2},{5,3},{10,12},{11,13},{12,10},{13,11},{18,20},{1... | collective-permute-start | bytes 3145736 | tf_op jit(solution)/shard_map/ppermute | solution.py:615
  424.7 28.9 %collective-permute-start.27 = (bf16[256,2048]{1,0:T(8,128)(2,1)S(1)}, bf16[256,2048]{1,0:T(8,128)(2,1)S(1)}, u32[]{:S(2)}, u32[]{:S(2)}) collective-permute-start(bf16[256,2048]{1,0:T(8,128)(2,1)S(1)} %get-tuple-element.242.refs_0_), channel_id=1, source_target_pairs={{0,2},{1,3},{6,4},{7,5},{8,10},{9,11},{14,12},{15,13},{16,18},{17,... | collective-permute-start | bytes 3145736 | tf_op jit(solution)/shard_map/ppermute | solution.py:615
  452.3 25.5 %collective-permute-start.32 = (bf16[256,2048]{1,0:T(8,128)(2,1)S(1)}, bf16[256,2048]{1,0:T(8,128)(2,1)S(1)}, u32[]{:S(2)}, u32[]{:S(2)}) collective-permute-start(bf16[256,2048]{1,0:T(8,128)(2,1)S(1)} %get-tuple-element.251.refs_1_), channel_id=1, source_target_pairs={{2,0},{3,1},{4,6},{5,7},{10,8},{11,9},{12,14},{13,15},{18,16},{19,... | collective-permute-start | bytes 3145736 | tf_op jit(solution)/shard_map/ppermute | solution.py:615
  453.9 26.1 %collective-permute-start.31 = (bf16[256,2048]{1,0:T(8,128)(2,1)S(1)}, bf16[256,2048]{1,0:T(8,128)(2,1)S(1)}, u32[]{:S(2)}, u32[]{:S(2)}) collective-permute-start(bf16[256,2048]{1,0:T(8,128)(2,1)S(1)} %get-tuple-element.250.refs_1_), channel_id=1, source_target_pairs={{2,4},{3,5},{4,2},{5,3},{10,12},{11,13},{12,10},{13,11},{18,20},{1... | collective-permute-start | bytes 3145736 | tf_op jit(solution)/shard_map/ppermute | solution.py:615
  455.2 27.5 %collective-permute-start.30 = (bf16[256,2048]{1,0:T(8,128)(2,1)S(1)}, bf16[256,2048]{1,0:T(8,128)(2,1)S(1)}, u32[]{:S(2)}, u32[]{:S(2)}) collective-permute-start(bf16[256,2048]{1,0:T(8,128)(2,1)S(1)} %get-tuple-element.249.refs_0_), channel_id=1, source_target_pairs={{0,2},{1,3},{6,4},{7,5},{8,10},{9,11},{14,12},{15,13},{16,18},{17,... | collective-permute-start | bytes 3145736 | tf_op jit(solution)/shard_map/ppermute | solution.py:615
  481.3 25.3 %collective-permute-start.35 = (bf16[256,2048]{1,0:T(8,128)(2,1)S(1)}, bf16[256,2048]{1,0:T(8,128)(2,1)S(1)}, u32[]{:S(2)}, u32[]{:S(2)}) collective-permute-start(bf16[256,2048]{1,0:T(8,128)(2,1)S(1)} %get-tuple-element.258.refs_1_), channel_id=1, source_target_pairs={{2,0},{3,1},{4,6},{5,7},{10,8},{11,9},{12,14},{13,15},{18,16},{19,... | collective-permute-start | bytes 3145736 | tf_op jit(solution)/shard_map/ppermute | solution.py:615
  482.9 26.1 %collective-permute-start.34 = (bf16[256,2048]{1,0:T(8,128)(2,1)S(1)}, bf16[256,2048]{1,0:T(8,128)(2,1)S(1)}, u32[]{:S(2)}, u32[]{:S(2)}) collective-permute-start(bf16[256,2048]{1,0:T(8,128)(2,1)S(1)} %get-tuple-element.257.refs_1_), channel_id=1, source_target_pairs={{2,4},{3,5},{4,2},{5,3},{10,12},{11,13},{12,10},{13,11},{18,20},{1... | collective-permute-start | bytes 3145736 | tf_op jit(solution)/shard_map/ppermute | solution.py:615
  510.4 25.4 %collective-permute-start.37 = (bf16[256,2048]{1,0:T(8,128)(2,1)S(1)}, bf16[256,2048]{1,0:T(8,128)(2,1)S(1)}, u32[]{:S(2)}, u32[]{:S(2)}) collective-permute-start(bf16[256,2048]{1,0:T(8,128)(2,1)S(1)} %get-tuple-element.264.refs_1_), channel_id=1, source_target_pairs={{2,0},{3,1},{4,6},{5,7},{10,8},{11,9},{12,14},{13,15},{18,16},{19,... | collective-permute-start | bytes 3145736 | tf_op jit(solution)/shard_map/ppermute | solution.py:615
  (58 other events, 550.6 us)
Sparse Core Ops, SparseCore 0:
  140.5 25.5 reduce-scatter.9
  300.3 23.0 reduce-scatter.5
  326.3 52.8 reduce-scatter.13
  382.4 43.9 reduce-scatter.7
  429.5 52.6 reduce-scatter.11
